TPU v7x, 256 devices: a whole 4x4x8 slice. The times are simulated.
256 devices in a mesh: dp: 8 (over x, core), space: 8 (over y, z_lo), chan: 4 (over z_hi).
Axes of the slice: x: 4, y: 4, z: 8 (z_hi: 4, z_lo: 2; z = z_hi * 2 + z_lo), core: 2. Of those that a mesh axis runs over, the one named last changes fastest.
Arguments:
- inputs: bfloat16 [8, 64, 16, 8, 128], P('dp', 'chan', 'space'), may hold values from -6 to 6
- pre_one: bfloat16 [8, 128, 16, 8, 128], P('dp', 'chan', 'space'), may hold values from -6 to 6
- pre_two: bfloat16 [8, 128, 16, 8, 128], P('dp', 'chan', 'space'), may hold values from -6 to 6
- grad_out: bfloat16 [8, 128, 16, 8, 128], P('dp', 'chan', 'space'), may hold values from -6 to 6
- weight_one: bfloat16 [128, 27, 64], P('chan'), may hold values from -0.21875 to 0.21875
- weight_two: bfloat16 [128, 27, 128], P('chan'), may hold values from -0.125 to 0.125
Outputs:
- grad_input: bfloat16 [8, 64, 16, 8, 128], P('dp', 'chan', 'space')
- grad_weight_one: float32 [128, 27, 64], P('chan')
- grad_weight_two: float32 [128, 27, 128], P('chan')
All inputs are finite; a program needn't handle non-finite values.
Results may differ from a plain program's by a relative error of at most 0.0049.
Values may be sent and summed in bfloat16 or wider, within the bound.
No kernel may reach another device: no remote copies, remote signals or barrier semaphores. Data moves between devices by JAX's collectives and lax.ppermute only.
A program may use at most 64 MiB of HBM per device.

v0:
```python
import jax
import jax.numpy as jnp
from jax import lax
from jax.sharding import PartitionSpec as P


def padded_2(block, sides, width):
    for axis, dim in sides:
        count = lax.axis_size(axis)
        forward = [(i, i + 1) for i in range(count - 1)]
        backward = [(target, source) for source, target in forward]
        low = lax.ppermute(
            lax.slice_in_dim(block, block.shape[dim] - width, None, axis=dim), axis, forward
        )
        high = lax.ppermute(lax.slice_in_dim(block, 0, width, axis=dim), axis, backward)
        block = jnp.concatenate([low, block, high], axis=dim)
    return block


def pad_sides(field):
    return jnp.pad(field, ((0, 0), (0, 0), (1, 1), (1, 1)))


def data_gradient(delta_pad, weights):
    out_ch = weights.shape[0]
    in_ch = weights.shape[2]
    kernel = weights.reshape(out_ch, 3, 3, 3, in_ch)[:, ::-1, ::-1, ::-1, :].transpose(
        4, 0, 1, 2, 3
    )
    result = lax.conv_general_dilated(
        pad_sides(delta_pad)[None],
        kernel,
        (1, 1, 1),
        "VALID",
        dimension_numbers=("NCDHW", "OIDHW", "NCDHW"),
        preferred_element_type=jnp.float32,
    )
    return result[0]


def tap_products(fixed, padded, starts):
    size_x = fixed.shape[1]
    size_y = fixed.shape[2]
    size_z = fixed.shape[3]
    blocks = []
    for first in range(3):
        for second in range(3):
            for third in range(3):
                sx, sy, sz = starts(first, second, third)
                window = padded[:, sx : sx + size_x, sy : sy + size_y, sz : sz + size_z]
                blocks.append(
                    jnp.einsum("oxyz,ixyz->oi", fixed, window, preferred_element_type=jnp.float32)
                )
    return jnp.stack(blocks, axis=1)


def filter_from_activations(activation_pad, delta):
    return tap_products(delta, pad_sides(activation_pad), lambda a, b, c: (a, b, c))


def local(inputs, pre_one, pre_two, grad_out, weight_one, weight_two):
    layer_input = inputs[0]
    pre_first = pre_one[0]
    pre_second = pre_two[0]
    upstream = grad_out[0]
    delta_two = jnp.where(pre_second > 0, upstream, jnp.zeros_like(upstream))
    hidden = jnp.maximum(pre_first, jnp.zeros_like(pre_first))
    delta_two_pad = padded_2(delta_two, (("space", 1),), 1)
    hidden_source = padded_2(hidden, (("space", 1),), 1)
    grad_two_local = filter_from_activations(
        lax.all_gather(hidden_source, "chan", axis=0, tiled=True), delta_two
    )
    hidden_grad = lax.psum_scatter(
        data_gradient(delta_two_pad, weight_two), "chan", scatter_dimension=0, tiled=True
    )
    delta_one = jnp.where(pre_first > 0, hidden_grad, jnp.zeros_like(hidden_grad)).astype(
        jnp.bfloat16
    )
    delta_one_pad = padded_2(delta_one, (("space", 1),), 1)
    input_source = padded_2(layer_input, (("space", 1),), 1)
    grad_one_local = filter_from_activations(
        lax.all_gather(input_source, "chan", axis=0, tiled=True), delta_one
    )
    input_grad = lax.psum_scatter(
        data_gradient(delta_one_pad, weight_one), "chan", scatter_dimension=0, tiled=True
    )
    grad_weight_one, grad_weight_two = lax.psum((grad_one_local, grad_two_local), ("dp", "space"))
    return (input_grad[None].astype(jnp.bfloat16), grad_weight_one, grad_weight_two)


def solution(mesh):
    return jax.shard_map(
        local,
        mesh=mesh,
        in_specs=(
            P("dp", "chan", "space", None, None),
            P("dp", "chan", "space", None, None),
            P("dp", "chan", "space", None, None),
            P("dp", "chan", "space", None, None),
            P("chan", None, None),
            P("chan", None, None),
        ),
        out_specs=(
            P("dp", "chan", "space", None, None),
            P("chan", None, None),
            P("chan", None, None),
        ),
        check_vma=False,
    )
```

profile of v0, /device:TPU:1, one launch (start us, length us, event | category | flops | bytes accessed | tf_op | source)
XLA Modules:
  0.0 702.6 jit_solution(18401356910911914634)
XLA Ops:
  7.2 1.0 maximum_bitcast_fusion
  8.3 1.3 collective-permute-start.7
  9.6 5.0 collective-permute-start.6
  14.6 0.9 copy.106
  15.5 0.4 collective-permute-done.6
  15.9 0.7 pad_maximum_fusion
  16.7 1.3 collective-permute-start.5
  18.0 4.9 collective-permute-start.4
  23.0 1.3 collective-permute-start.1
  24.3 5.2 collective-permute-start
  29.6 21.6 %all_gather.6 = bf16[64,4,8,128]{3,0,2,1:T(8,128)(2,1)S(1)} all-gather(bf16[16,4,8,128]{3,0,2,1:T(8,128)(2,1)S(1)} %pad_maximum_fusion.1), channel_id=1, replica_groups=mesh['dp'=8,'space'=8,'chan'=4] {'chan'}, dimensions={0}, use_global_device_ids=true | all-gather | bytes 655360 | tf_op jit(solution)/shard_map/all_gather | solution.py:82
  51.5 2.1 copy.99
  53.5 0.7 pad.19.clone
  54.5 0.4 copy-done.8
  54.9 1.8 fusion.19
  57.0 1.3 copy.98
  58.5 4.0 all-gather.2.cloned.1.call-done
  62.5 1.4 fusion.51
  63.9 0.3 fusion.50
  64.2 0.4 fusion.49
  64.6 0.4 fusion.48
  65.2 0.4 fusion.46
  65.6 0.4 fusion.45
  66.2 0.4 fusion.43
  66.6 0.4 fusion.42
  67.2 0.4 fusion.40
  67.6 0.4 fusion.39
  68.2 0.4 fusion.37
  68.6 0.4 fusion.36
  69.3 0.4 fusion.34
  69.6 0.4 fusion.33
  70.3 0.4 fusion.31
  70.6 0.4 fusion.30
  71.3 0.4 fusion.28
  71.7 0.4 fusion.27
  72.3 0.4 fusion.25
  72.7 29.2 %reduce-scatter.3.cloned.1.call-done = f32[32,2,8,128]{3,0,2,1:T(8,128)} async-done(((f32[128,2,8,128]{3,0,2,1:T(8,128)}), f32[32,2,8,128]{3,0,2,1:T(8,128)}) %reduce-scatter.3.cloned.1.call-update) | async-done | bytes 262160 | tf_op jit(solution)/shard_map/reduce_scatter | solution.py:73
  101.9 1.0 select_convert_fusion
  102.9 1.3 collective-permute-start.3
  104.2 4.2 collective-permute-start.2
  108.9 0.3 fusion.76
  109.6 0.3 fusion.73
  109.9 0.3 fusion.72
  110.4 0.3 fusion.70
  111.4 0.3 fusion.66
  111.9 0.3 fusion.64
  112.7 0.3 fusion.61
  113.7 0.3 fusion.57
  114.0 0.7 copy-done.4
  115.0 2.1 copy.100
  117.1 0.7 pad.21.clone
  118.1 0.7 copy-done.7
  118.8 1.8 fusion.16
  120.9 1.2 copy.41
  122.2 0.8 fusion.56
  123.0 0.9 fusion.55
  123.8 0.9 fusion.54
  124.7 0.8 fusion.53
  125.5 0.9 fusion.52
  126.4 22.5 %reduce-scatter.5.cloned.1.call-done = f32[16,2,8,128]{3,2,1,0:T(8,128)} async-done(((f32[64,2,8,128]{3,2,1,0:T(8,128)}), f32[16,2,8,128]{3,2,1,0:T(8,128)}) %reduce-scatter.5.cloned.1.call-update) | async-done | bytes 131088 | tf_op jit(solution)/shard_map/reduce_scatter | solution.py:84
  148.9 1.5 convert_bitcast_fusion
  150.5 542.0 %all-reduce.7.cloned.1.call-done = (f32[32,27,64]{2,0,1:T(8,128)}, f32[32,27,128]{2,0,1:T(8,128)}) async-done(((f32[32,27,64]{2,0,1:T(8,128)}, f32[32,27,128]{2,0,1:T(8,128)}), (f32[32,27,64]{2,0,1:T(8,128)}, f32[32,27,128]{2,0,1:T(8,128)})) %all-reduce.7.cloned.1.call-update) | async-done | bytes 663568 | tf_op jit(solution)/shard_map/psum | solution.py:87
  692.5 1.8 copy.161
  694.3 1.8 copy.162
  (68 shorter events, 7.4 us)
Async XLA Ops:
  7.2 47.4 %copy-start = (bf16[32,27,128]{2,0,1:T(8,128)(2,1)S(1)}, bf16[32,27,128]{2,0,1:T(8,128)(2,1)}, u32[]{:S(2)}) copy-start(bf16[32,27,128]{2,0,1:T(8,128)(2,1)} %param.11) | copy-start | bytes 663556
  7.2 15.8 %copy-start.5 = (bf16[1,32,2,8,128]{4,3,2,1,0:T(8,128)(2,1)S(1)}, bf16[1,32,2,8,128]{4,3,2,1,0:T(8,128)(2,1)}, u32[]{:S(2)}) copy-start(bf16[1,32,2,8,128]{4,3,2,1,0:T(8,128)(2,1)} %param.9) | copy-start | bytes 393220
  7.2 15.8 %copy-start.6 = (bf16[1,32,2,8,128]{4,3,2,1,0:T(8,128)(2,1)S(1)}, bf16[1,32,2,8,128]{4,3,2,1,0:T(8,128)(2,1)}, u32[]{:S(2)}) copy-start(bf16[1,32,2,8,128]{4,3,2,1,0:T(8,128)(2,1)} %param.8) | copy-start | bytes 393220
  7.2 55.3 %all-gather.2.cloned.1.call-start = ((), (), s32[]{:S(2)}) async-start(), calls=%async_computation.4 | async-start | bytes 1310720 | tf_op jit(solution)/shard_map/all_gather | solution.py:71
  8.3 7.2 %collective-permute-start.7 = (bf16[32,1,8,128]{3,0,2,1:T(8,128)(2,1)S(1)}, bf16[32,1,8,128]{3,0,2,1:T(8,128)(2,1)S(1)}, u32[]{:S(2)}, u32[]{:S(2)}) collective-permute-start(bf16[32,1,8,128]{3,0,2,1:T(8,128)(2,1)S(1)} %get-tuple-element.9), channel_id=1, source_target_pairs={{4,0},{8,4},{12,8},{16,12},{20,16},{24,20},{28,24},{5,1},{9,5},{13... | collective-permute-start | bytes 196616 | tf_op jit(solution)/shard_map/ppermute | solution.py:15
  9.6 6.3 collective-permute-start.6
  16.7 85.2 %reduce-scatter.3.cloned.1.call-start = ((), (), s32[]{:S(2)}) async-start(), calls=%async_computation.2 | async-start | bytes 1310720 | tf_op jit(solution)/shard_map/reduce_scatter | solution.py:73
  16.7 12.8 %collective-permute-start.5 = (bf16[16,1,8,128]{3,0,2,1:T(8,128)(2,1)S(1)}, bf16[16,1,8,128]{3,0,2,1:T(8,128)(2,1)S(1)}, u32[]{:S(2)}, u32[]{:S(2)}) collective-permute-start(bf16[16,1,8,128]{3,0,2,1:T(8,128)(2,1)S(1)} %get-tuple-element.15), channel_id=1, source_target_pairs={{4,0},{8,4},{12,8},{16,12},{20,16},{24,20},{28,24},{5,1},{9,5},{13... | collective-permute-start | bytes 98312 | tf_op jit(solution)/shard_map/ppermute | solution.py:15
  18.0 11.5 %collective-permute-start.4 = (bf16[16,1,8,128]{3,0,2,1:T(8,128)(2,1)S(1)}, bf16[16,1,8,128]{3,0,2,1:T(8,128)(2,1)S(1)}, u32[]{:S(2)}, u32[]{:S(2)}) collective-permute-start(bf16[16,1,8,128]{3,0,2,1:T(8,128)(2,1)S(1)} %get-tuple-element.14), channel_id=1, source_target_pairs={{0,4},{4,8},{8,12},{12,16},{16,20},{20,24},{24,28},{1,5},{5,9},{9,... | collective-permute-start | bytes 98312 | tf_op jit(solution)/shard_map/ppermute | solution.py:12
  23.0 28.1 %collective-permute-start.1 = (bf16[32,1,8,128]{3,0,2,1:T(8,128)(2,1)S(1)}, bf16[32,1,8,128]{3,0,2,1:T(8,128)(2,1)S(1)}, u32[]{:S(2)}, u32[]{:S(2)}) collective-permute-start(bf16[32,1,8,128]{3,0,2,1:T(8,128)(2,1)S(1)} %get-tuple-element.13), channel_id=1, source_target_pairs={{4,0},{8,4},{12,8},{16,12},{20,16},{24,20},{28,24},{5,1},{9,5},{13... | collective-permute-start | bytes 196616 | tf_op jit(solution)/shard_map/ppermute | solution.py:15
  24.3 26.9 %collective-permute-start = (bf16[32,1,8,128]{3,0,2,1:T(8,128)(2,1)S(1)}, bf16[32,1,8,128]{3,0,2,1:T(8,128)(2,1)S(1)}, u32[]{:S(2)}, u32[]{:S(2)}) collective-permute-start(bf16[32,1,8,128]{3,0,2,1:T(8,128)(2,1)S(1)} %get-tuple-element.12), channel_id=1, source_target_pairs={{0,4},{4,8},{8,12},{12,16},{16,20},{20,24},{24,28},{1,5},{5,9},{9,... | collective-permute-start | bytes 196616 | tf_op jit(solution)/shard_map/ppermute | solution.py:12
  54.3 0.7 copy-start.8
  58.4 90.5 %reduce-scatter.5.cloned.1.call-start = ((), (), s32[]{:S(2)}) async-start(), calls=%async_computation.3 | async-start | bytes 655360 | tf_op jit(solution)/shard_map/reduce_scatter | solution.py:84
  62.5 1.4 copy-start.1
  72.0 29.9 %copy-start.2 = (bf16[1,32,2,8,128]{4,3,2,1,0:T(8,128)(2,1)S(1)}, bf16[1,32,2,8,128]{4,3,2,1,0:T(8,128)(2,1)}, u32[]{:S(2)}) copy-start(bf16[1,32,2,8,128]{4,3,2,1,0:T(8,128)(2,1)} %param.7) | copy-start | bytes 393220
  72.7 36.5 %copy-start.3 = (f32[32,27,128]{2,0,1:T(8,128)}, f32[32,27,128]{2,0,1:T(8,128)S(1)}, u32[]{:S(2)}) copy-start(f32[32,27,128]{2,0,1:T(8,128)S(1)} %fusion.25) | copy-start | bytes 1327108
  102.9 11.1 %collective-permute-start.3 = (bf16[32,1,8,128]{3,0,2,1:T(8,128)(2,1)S(1)}, bf16[32,1,8,128]{3,0,2,1:T(8,128)(2,1)S(1)}, u32[]{:S(2)}, u32[]{:S(2)}) collective-permute-start(bf16[32,1,8,128]{3,0,2,1:T(8,128)(2,1)S(1)} %get-tuple-element.11), channel_id=1, source_target_pairs={{4,0},{8,4},{12,8},{16,12},{20,16},{24,20},{28,24},{5,1},{9,5},{13... | collective-permute-start | bytes 196616 | tf_op jit(solution)/shard_map/ppermute | solution.py:15
  104.2 9.8 %collective-permute-start.2 = (bf16[32,1,8,128]{3,0,2,1:T(8,128)(2,1)S(1)}, bf16[32,1,8,128]{3,0,2,1:T(8,128)(2,1)S(1)}, u32[]{:S(2)}, u32[]{:S(2)}) collective-permute-start(bf16[32,1,8,128]{3,0,2,1:T(8,128)(2,1)S(1)} %get-tuple-element.10), channel_id=1, source_target_pairs={{0,4},{4,8},{8,12},{12,16},{16,20},{20,24},{24,28},{1,5},{5,9},{9,... | collective-permute-start | bytes 196616 | tf_op jit(solution)/shard_map/ppermute | solution.py:12
  114.0 0.8 copy-start.4
  117.8 0.9 copy-start.7
  122.1 570.4 %all-reduce.7.cloned.1.call-start = ((), (), s32[]{:S(2)}) async-start(), calls=%async_computation.5 | async-start | bytes 1769472 | tf_op jit(solution)/shard_map/psum | solution.py:87
Sparse Core Ops, SparseCore 0:
  16.8 45.6 all-gather.1
  65.0 36.8 reduce-scatter.2
  122.2 26.6 reduce-scatter.4
  152.3 540.1 all-reduce.6
where the time goes:
time: 704 us; the launch traced here: 703 us
  waiting for transfers between devices  598 us (85%)
  starting transfers between devices  24.6 us (3%)
  matrix products  23.6 us (3%)
  blocking collectives  21.6 us (3%)
  local copies, waits for them, and re-layouts  15.6 us (2%)
  between operations  14.2 us (2%)
    psum x1, waiting for transfers between devices, local(): lax.psum((grad_one_local, grad_two_local), ('dp', 'space'))  542 us
    reduce_scatter x1, waiting for transfers between devices, local(): lax.psum_scatter(data_gradient(delta_two_pad, weight_two), 'chan', scatte...  29.2 us
    reduce_scatter x1, waiting for transfers between devices, local(): lax.psum_scatter(data_gradient(delta_one_pad, weight_one), 'chan', scatte...  22.5 us
    all_gather x1, blocking collectives, local(): lax.all_gather(input_source, 'chan', axis=0, tiled=True)  21.6 us
    dot_general x54, matrix products, tap_products(): jnp.einsum('oxyz,ixyz->oi', fixed, window, preferred_element_type=jnp.flo...  20 us
    ppermute x4, starting transfers between devices, padded_2(): lax.ppermute(lax.slice_in_dim(block, block.shape[dim] - width, None, axis...  19.3 us
  transfers between devices with their start and end apart: 12, of which 5 were waited for; matrix products, arithmetic and copies ran while one was open for 4% of the time, Pallas kernels for 0%

commit v1 on v0

v1 whole, which is shorter than its diff:
```python
import jax
import jax.numpy as jnp
from jax import lax
from jax.experimental import pallas as pl
from jax.experimental.pallas import tpu as pltpu
from jax.sharding import PartitionSpec as P

TAPS = 27
ROWS = 32
CELLS = 16
LANES = 128
DEPTH = TAPS * ROWS
CHUNK = 24
PARAMS = pltpu.CompilerParams(vmem_limit_bytes=40 * 1024 * 1024)


def fill_patches(patches, low, own, high):
    lane = lax.broadcasted_iota(jnp.int32, (ROWS, LANES), 1)
    first = lane == 0
    last = lane == LANES - 1
    empty = jnp.zeros((ROWS, LANES), jnp.bfloat16)

    def put(a, b, c, x, y, value):
        row = ((a * 3 + b) * 3 + c) * ROWS
        column = (x * 8 + y) * LANES
        patches[row : row + ROWS, column : column + LANES] = value

    for plane in range(4):
        for y in range(8):
            if plane == 0:
                block = low[y]
            elif plane == 3:
                block = high[y]
            else:
                block = own[(plane - 1) * 8 + y]
            wide = block.astype(jnp.float32)
            after = jnp.where(first, 0.0, pltpu.roll(wide, 1, 1)).astype(jnp.bfloat16)
            before = jnp.where(last, 0.0, pltpu.roll(wide, LANES - 1, 1)).astype(jnp.bfloat16)
            for c, value in enumerate((after, block, before)):
                for a in range(3):
                    x = plane - a
                    if x < 0 or x > 1:
                        continue
                    for b in range(3):
                        target = y + 1 - b
                        if 0 <= target < 8:
                            put(a, b, c, x, target, value)
    for a in range(3):
        for c in range(3):
            for x in range(2):
                put(a, 0, c, x, 0, empty)
                put(a, 2, c, x, 7, empty)


def data_two_kernel(low, own, high, weight, out, patches):
    fill_patches(patches, low, own, high)
    for group in range(4):
        columns = slice(group * 512, group * 512 + 512)
        result = jnp.dot(weight[...], patches[:, columns], preferred_element_type=jnp.float32)
        result = result.astype(jnp.bfloat16)
        for part in range(4):
            for cell in range(4):
                out[part, group * 4 + cell] = result[
                    part * 32 : part * 32 + 32, cell * LANES : cell * LANES + LANES
                ]


def lay_out(fields, source, start, count):
    for part in range(4):
        for cell in range(CELLS):
            fields[part * count : part * count + count, cell * LANES : cell * LANES + LANES] = source[
                part, cell, start : start + count
            ]


def tap_sums(patches, fields):
    sums = lax.dot_general(
        patches[...], fields[...], (((1,), (1,)), ((), ())), preferred_element_type=jnp.float32
    )
    return jnp.concatenate(
        [sums[(TAPS - 1 - k) * ROWS : (TAPS - k) * ROWS] for k in range(TAPS)], axis=0
    )


def filter_two_kernel(low, own, high, gathered, out, patches, fields):
    fill_patches(patches, low, own, high)
    lay_out(fields, gathered, 0, 32)
    out[...] = tap_sums(patches, fields).astype(jnp.bfloat16)


def layer_one_kernel(low, own, high, gathered, weight, filter_two, grad, sums, patches, fields):
    fill_patches(patches, low, own, high)
    lay_out(fields, gathered, 32, 16)
    for group in range(4):
        columns = slice(group * 512, group * 512 + 512)
        result = jnp.dot(weight[...], patches[:, columns], preferred_element_type=jnp.float32)
        for part in range(4):
            for cell in range(4):
                grad[part, group * 4 + cell] = result[
                    part * 16 : part * 16 + 16, cell * LANES : cell * LANES + LANES
                ]
    one = tap_sums(patches, fields)
    half = DEPTH // 2
    sums[0:DEPTH] = filter_two[...]
    sums[DEPTH : DEPTH + half] = jnp.concatenate([one[:half], one[half:]], axis=1).astype(jnp.bfloat16)
    sums[DEPTH + half :] = jnp.zeros((64 * CHUNK - DEPTH - half, LANES), jnp.bfloat16)


def call(kernel, outs, scratch, flops):
    return pl.pallas_call(
        kernel,
        out_shape=outs,
        scratch_shapes=scratch,
        compiler_params=PARAMS,
        cost_estimate=pl.CostEstimate(flops=flops, bytes_accessed=1 << 20, transcendentals=0),
    )


def by_rows(field):
    moved = field[0].transpose(1, 2, 0, 3)
    return moved.reshape((CELLS,) + moved.shape[2:])


def neighbours(field):
    count = lax.axis_size("space")
    forward = [(i, i + 1) for i in range(count - 1)]
    backward = [(i + 1, i) for i in range(count - 1)]
    low = lax.ppermute(field[8:], "space", forward)
    high = lax.ppermute(field[:8], "space", backward)
    return low, high


def flipped(weights):
    return weights[:, ::-1, :].transpose(2, 1, 0).reshape(weights.shape[2], DEPTH)


def local(inputs, pre_one, pre_two, grad_out, weight_one, weight_two):
    bf16 = jnp.bfloat16
    patches = pltpu.VMEM((DEPTH, CELLS * LANES), bf16)
    delta_two = by_rows(jnp.where(pre_two > 0, grad_out, jnp.zeros_like(grad_out)))
    low_two, high_two = neighbours(delta_two)
    pre_rows = by_rows(pre_one)
    hidden = jnp.maximum(pre_rows, jnp.zeros_like(pre_rows))
    both = jnp.concatenate([hidden, by_rows(inputs), jnp.zeros((CELLS, 16, LANES), bf16)], axis=1)
    gathered = lax.all_gather(both, "chan", axis=0, tiled=False)

    partial_two = call(
        data_two_kernel, jax.ShapeDtypeStruct((4, CELLS, 32, LANES), bf16), [patches], 500_000_000
    )(low_two, delta_two, high_two, flipped(weight_two))
    parts = lax.all_to_all(partial_two, "chan", 0, 0, tiled=True)
    hidden_grad = jnp.sum(parts.astype(jnp.float32), axis=0)
    delta_one = jnp.where(pre_rows > 0, hidden_grad, jnp.zeros_like(hidden_grad)).astype(bf16)
    low_one, high_one = neighbours(delta_one)

    filter_two = call(
        filter_two_kernel,
        jax.ShapeDtypeStruct((DEPTH, LANES), bf16),
        [patches, pltpu.VMEM((128, CELLS * LANES), bf16)],
        500_000_000,
    )(low_two, delta_two, high_two, gathered)

    grad, sums = call(
        layer_one_kernel,
        (
            jax.ShapeDtypeStruct((4, CELLS, 16, LANES), jnp.float32),
            jax.ShapeDtypeStruct((64 * CHUNK, LANES), bf16),
        ),
        [patches, pltpu.VMEM((64, CELLS * LANES), bf16)],
        500_000_000,
    )(low_one, delta_one, high_one, gathered, flipped(weight_one), filter_two)

    input_grad = lax.psum_scatter(grad, "chan", scatter_dimension=0, tiled=True)[0]
    input_grad = input_grad.reshape(2, 8, 16, LANES).transpose(2, 0, 1, 3)[None].astype(bf16)

    every = ("dp", "space")
    pieces = lax.all_to_all(sums.reshape(64, CHUNK, LANES), every, 0, 0, tiled=True)
    piece = jnp.sum(pieces.astype(jnp.float32), axis=0).astype(bf16)
    copies = jnp.broadcast_to(piece[None], (64, CHUNK, LANES))
    total = lax.all_to_all(copies, every, 0, 0, tiled=True).reshape(64 * CHUNK, LANES)
    total = total.astype(jnp.float32)
    half = DEPTH // 2
    grad_two = total[:DEPTH].reshape(TAPS, ROWS, LANES).transpose(1, 0, 2)
    one = total[DEPTH : DEPTH + half]
    one = jnp.concatenate([one[:, :64], one[:, 64:]], axis=0)
    grad_one = one.reshape(TAPS, ROWS, 64).transpose(1, 0, 2)
    return input_grad, grad_one, grad_two


def solution(mesh):
    field = P("dp", "chan", "space", None, None)
    weight = P("chan", None, None)
    return jax.shard_map(
        local,
        mesh=mesh,
        in_specs=(field, field, field, field, weight, weight),
        out_specs=(field, weight, weight),
        check_vma=False,
    )
```

time: 704 us -> 123 us (0.17)
  waiting for transfers between devices: 598 us -> 51.9 us
  matrix products: 23.6 us -> 0 us
  blocking collectives: 21.6 us -> 0 us
  starting transfers between devices: 24.6 us -> 41.6 us
  local copies, waits for them, and re-layouts: 15.6 us -> 5.87 us
    psum x1 -> x0, waiting for transfers between devices: 542 us -> none  [local(): lax.psum((grad_one_local, grad_two_local), ('dp', 'space'))]
    reduce_scatter x2 -> x1, waiting for transfers between devices: 51.7 us -> 11.9 us  [local(): lax.psum_scatter(grad, 'chan', scatter_dimension=0, tiled=True)[0]]
    all_to_all x0 -> x3, waiting for transfers between devices: none -> 37.9 us  [the longest x1 25.3 us: local(): parts = lax.all_to_all(partial_two, 'chan', 0, 0, tiled=True)]
    all_to_all x0 -> x3, starting transfers between devices: none -> 29.7 us  [the longest x1 17.1 us: local(): lax.all_to_all(sums.reshape(64, CHUNK, LANES), every, 0, 0, tiled=True)]
    all_gather x1 -> x0, blocking collectives: 21.6 us -> none  [local(): lax.all_gather(input_source, 'chan', axis=0, tiled=True)]
    dot_general x54 -> x0, matrix products: 20 us -> none  [tap_products(): jnp.einsum('oxyz,ixyz->oi', fixed, window, preferred_element_type=jnp.flo...]
    ppermute x8 -> x4, starting transfers between devices: 24.4 us -> 11.8 us  [the longest x2 8.99 us: neighbours(): low = lax.ppermute(field[8:], 'space', forward)]
    unnamed x24 -> x14, local copies, waits for them, and re-layouts: 11.9 us -> 2.19 us
  transfers between devices with their start and end apart: 12 -> 9, of which waited for: 5 -> 6; matrix products, arithmetic and copies ran while one was open for 4% -> 2% of each run, Pallas kernels for 0% -> 3%
where the time goes in v1:
time: 123 us; the launch traced here: 122 us
  waiting for transfers between devices  51.9 us (42%)
  starting transfers between devices  41.6 us (34%)
  between operations  14.3 us (12%)
  Pallas kernels  5.9 us (5%)
  local copies, waits for them, and re-layouts  5.87 us (5%)
  other arithmetic  2.95 us (2%)
    all_to_all x1, waiting for transfers between devices, local(): parts = lax.all_to_all(partial_two, 'chan', 0, 0, tiled=True)  25.3 us
    all_to_all x1, starting transfers between devices, local(): lax.all_to_all(sums.reshape(64, CHUNK, LANES), every, 0, 0, tiled=True)  17.1 us
    reduce_scatter x1, waiting for transfers between devices, local(): lax.psum_scatter(grad, 'chan', scatter_dimension=0, tiled=True)[0]  11.9 us
    all_to_all x1, waiting for transfers between devices, local(): lax.all_to_all(sums.reshape(64, CHUNK, LANES), every, 0, 0, tiled=True)  10.3 us
    ppermute x2, starting transfers between devices, neighbours(): low = lax.ppermute(field[8:], 'space', forward)  8.99 us
    all_to_all x1, starting transfers between devices, local(): parts = lax.all_to_all(partial_two, 'chan', 0, 0, tiled=True)  7.98 us
    all_to_all x1, starting transfers between devices, local(): lax.all_to_all(copies, every, 0, 0, tiled=True).reshape(64 * CHUNK, LANES)  4.53 us
    ppermute x2, starting transfers between devices, neighbours(): high = lax.ppermute(field[:8], 'space', backward)  2.85 us
  transfers between devices with their start and end apart: 9, of which 6 were waited for; matrix products, arithmetic and copies ran while one was open for 2% of the time, Pallas kernels for 3%

profile of v1, /device:TPU:1, one launch (start us, length us, event | category | flops | bytes accessed | tf_op | source)
XLA Modules:
  0.0 122.4 jit_solution(1259029322652265184)
XLA Ops:
  7.2 0.0 copy-start.2
  7.2 0.0 all-gather.3.cloned.1.call-start
  7.2 0.9 copy.30
  8.1 0.0 copy-done.2
  8.2 0.1 pad.4.clone
  8.2 0.8 maximum_maximum_fusion
  9.1 0.0 copy-start.5
  9.1 0.0 copy-start.6
  9.1 0.0 all-gather.3.cloned.1.call-update
  9.1 0.9 copy-done.5
  10.0 0.1 copy-done.6
  10.0 0.1 compare_select_fusion
  10.1 0.0 copy-start.3
  10.1 1.4 %collective-permute-start.1 = (bf16[8,32,128]{2,1,0:T(8,128)(2,1)S(1)}, bf16[8,32,128]{2,1,0:T(8,128)(2,1)S(1)}, u32[]{:S(2)}, u32[]{:S(2)}) collective-permute-start(bf16[8,32,128]{2,1,0:T(8,128)(2,1)S(1)} %get-tuple-element.11), channel_id=1, source_target_pairs={{4,0},{8,4},{12,8},{16,12},{20,16},{24,20},{28,24},{5,1},{9,5},{13... | collective-permute-start | bytes 196616 | tf_op jit(solution)/shard_map/ppermute | solution.py:129
  11.6 5.0 %collective-permute-start = (bf16[8,32,128]{2,1,0:T(8,128)(2,1)S(1)}, bf16[8,32,128]{2,1,0:T(8,128)(2,1)S(1)}, u32[]{:S(2)}, u32[]{:S(2)}) collective-permute-start(bf16[8,32,128]{2,1,0:T(8,128)(2,1)S(1)} %get-tuple-element.12), channel_id=1, source_target_pairs={{0,4},{4,8},{8,12},{12,16},{16,20},{20,24},{24,28},{1,5},{5,9},{9,... | collective-permute-start | bytes 196616 | tf_op jit(solution)/shard_map/ppermute | solution.py:128
  16.6 0.0 copy-done.3
  16.6 0.2 copy.28.weight
  16.8 0.0 collective-permute-done.1.high
  16.8 1.1 collective-permute-done.low
  17.9 1.8 %shard_map.85 = bf16[4,16,32,128]{3,2,1,0:T(8,128)(2,1)} custom-call(bf16[8,32,128]{2,1,0:T(8,128)(2,1)S(1)} %collective-permute-done.low, bf16[16,32,128]{2,1,0:T(8,128)(2,1)S(1)} %bitcast.46, bf16[8,32,128]{2,1,0:T(8,128)(2,1)S(1)} %collective-permute-done.1.high, bf16[128,864]{1,0:T(8,128)(2,1)S(1)} %copy.28.weight), custom_call_target="tpu_custom_call" | custom-call | flops 500000000 | bytes 1048576 | tf_op jit(solution)/shard_map/pallas_call | solution.py:147
  19.7 8.0 %all-to-all-start = ((bf16[4,16,32,128]{3,2,1,0:T(8,128)(2,1)}), bf16[4,16,32,128]{3,2,1,0:T(8,128)(2,1)S(1)}, u32[]{:S(2)}, u32[]{:S(2)}) async-start(bf16[4,16,32,128]{3,2,1,0:T(8,128)(2,1)} %shard_map.85), calls=%async_computation | async-start | bytes 1048576 | tf_op jit(solution)/shard_map/all_to_all | solution.py:150
  27.7 0.1 copy_compare_fusion
  27.8 25.3 %all-to-all-done = bf16[4,16,32,128]{3,2,1,0:T(8,128)(2,1)S(1)} async-done(((bf16[4,16,32,128]{3,2,1,0:T(8,128)(2,1)}), bf16[4,16,32,128]{3,2,1,0:T(8,128)(2,1)S(1)}, u32[]{:S(2)}, u32[]{:S(2)}) %all-to-all-start) | async-done | bytes 524320 | tf_op jit(solution)/shard_map/all_to_all | solution.py:150
  53.1 0.1 convert_reduce_fusion
  53.1 0.0 copy-start.4
  53.1 0.1 select_convert_fusion.own
  53.2 1.4 %collective-permute-start.3 = (bf16[8,32,128]{2,1,0:T(8,128)(2,1)S(1)}, bf16[8,32,128]{2,1,0:T(8,128)(2,1)S(1)}, u32[]{:S(2)}, u32[]{:S(2)}) collective-permute-start(bf16[8,32,128]{2,1,0:T(8,128)(2,1)S(1)} %get-tuple-element.9), channel_id=1, source_target_pairs={{4,0},{8,4},{12,8},{16,12},{20,16},{24,20},{28,24},{5,1},{9,5},{13... | collective-permute-start | bytes 196616 | tf_op jit(solution)/shard_map/ppermute | solution.py:129
  54.7 4.0 %collective-permute-start.2 = (bf16[8,32,128]{2,1,0:T(8,128)(2,1)S(1)}, bf16[8,32,128]{2,1,0:T(8,128)(2,1)S(1)}, u32[]{:S(2)}, u32[]{:S(2)}) collective-permute-start(bf16[8,32,128]{2,1,0:T(8,128)(2,1)S(1)} %get-tuple-element.10), channel_id=1, source_target_pairs={{0,4},{4,8},{8,12},{12,16},{16,20},{20,24},{24,28},{1,5},{5,9},{9,... | collective-permute-start | bytes 196616 | tf_op jit(solution)/shard_map/ppermute | solution.py:128
  58.7 0.0 copy-done.4
  58.7 0.1 copy.31.weight
  58.8 0.3 all-gather.3.cloned.1.call-done
  59.2 0.0 copy-start
  59.2 1.2 copy-done
  60.4 0.0 copy-start.1
  60.4 1.3 %shard_map.86.filter_two = bf16[864,128]{1,0:T(8,128)(2,1)S(1)} custom-call(bf16[8,32,128]{2,1,0:T(8,128)(2,1)S(1)} %collective-permute-done.low, bf16[16,32,128]{2,1,0:T(8,128)(2,1)S(1)} %bitcast.47, bf16[8,32,128]{2,1,0:T(8,128)(2,1)S(1)} %collective-permute-done.1.high, bf16[4,16,64,128]{3,2,1,0:T(8,128)(2,1)S(1)} %bitcast.48), custom_call_target="tpu_custom_call" | custom-call | flops 500000000 | bytes 1048576 | tf_op jit(solution)/shard_map/pallas_call | solution.py:155
  61.8 0.0 collective-permute-done.3.high
  61.8 0.0 collective-permute-done.2.low
  61.8 0.0 copy-done.1
  61.8 2.7 %shard_map.87 = (f32[4,16,16,128]{3,2,1,0:T(8,128)}, bf16[1536,128]{1,0:T(8,128)(2,1)}) custom-call(bf16[8,32,128]{2,1,0:T(8,128)(2,1)S(1)} %collective-permute-done.2.low, bf16[16,32,128]{2,1,0:T(8,128)(2,1)S(1)} %select_convert_fusion.own, bf16[8,32,128]{2,1,0:T(8,128)(2,1)S(1)} %collective-permute-done.3.high, bf16[4,16,64,128]{3,2,1,0:T(8,128)(2,1)S(1)} %bitcast.49, ...), custom_call_target="tpu_custom_call" | custom-call | flops 500000000 | bytes 1048576 | tf_op jit(solution)/shard_map/pallas_call | solution.py:162
  64.5 17.1 %all-to-all-start.1 = ((bf16[64,24,128]{2,1,0:T(8,128)(2,1)}), bf16[64,24,128]{2,1,0:T(8,128)(2,1)S(1)}, u32[]{:S(2)}, u32[]{:S(2)}) async-start(bf16[64,24,128]{2,1,0:T(8,128)(2,1)} %bitcast.24), calls=%async_computation.2 | async-start | bytes 786432 | tf_op jit(solution)/shard_map/all_to_all | solution.py:176
  81.7 0.0 reduce-scatter.2.cloned.1.call-start
  81.7 0.7 reduce-scatter.2.cloned.1.call-update
  82.4 10.3 %all-to-all-done.1 = bf16[64,24,128]{2,1,0:T(8,128)(2,1)S(1)} async-done(((bf16[64,24,128]{2,1,0:T(8,128)(2,1)}), bf16[64,24,128]{2,1,0:T(8,128)(2,1)S(1)}, u32[]{:S(2)}, u32[]{:S(2)}) %all-to-all-start.1) | async-done | bytes 393248 | tf_op jit(solution)/shard_map/all_to_all | solution.py:176
  92.8 0.1 reduce_sum.22
  92.9 0.8 broadcast_in_dim.15
  93.7 4.5 %all-to-all-start.2 = ((bf16[64,24,128]{2,1,0:T(8,128)(2,1)}), bf16[64,24,128]{2,1,0:T(8,128)(2,1)S(1)}, u32[]{:S(2)}, u32[]{:S(2)}) async-start(bf16[64,24,128]{2,1,0:T(8,128)(2,1)} %broadcast_in_dim.15), calls=%async_computation.3 | async-start | bytes 786432 | tf_op jit(solution)/shard_map/all_to_all | solution.py:179
  98.2 11.9 %reduce-scatter.2.cloned.1.call-done = f32[1,16,16,128]{3,2,1,0:T(8,128)} async-done(((f32[4,16,16,128]{3,2,1,0:T(8,128)}), f32[1,16,16,128]{3,2,1,0:T(8,128)}) %reduce-scatter.2.cloned.1.call-update) | async-done | bytes 131088 | tf_op jit(solution)/shard_map/reduce_scatter | solution.py:172
  110.1 0.9 convert_element_type.28
  111.0 0.6 copy.38
  111.6 2.2 %all-to-all-done.2 = bf16[64,24,128]{2,1,0:T(8,128)(2,1)S(1)} async-done(((bf16[64,24,128]{2,1,0:T(8,128)(2,1)}), bf16[64,24,128]{2,1,0:T(8,128)(2,1)S(1)}, u32[]{:S(2)}, u32[]{:S(2)}) %all-to-all-start.2) | async-done | bytes 393248 | tf_op jit(solution)/shard_map/all_to_all | solution.py:179
  113.8 0.1 convert_element_type.32
  113.9 0.1 fusion
  114.0 0.8 pad_maximum_fusion
  114.8 0.8 slice.46
  (6 shorter events, 0.1 us)
Async XLA Ops:
  7.2 0.9 copy-start.2
  7.2 52.0 %all-gather.3.cloned.1.call-start = ((), (), s32[]{:S(2)}) async-start(), calls=%async_computation.5 | async-start | bytes 1310720 | tf_op jit(solution)/shard_map/all_gather | solution.py:145
  9.1 0.9 copy-start.5
  9.1 1.0 copy-start.6
  10.1 6.5 %copy-start.3 = (bf16[32,27,128]{2,0,1:T(8,128)(2,1)S(1)}, bf16[32,27,128]{2,0,1:T(8,128)(2,1)}, u32[]{:S(2)}) copy-start(bf16[32,27,128]{2,0,1:T(8,128)(2,1)} %param.11) | copy-start | bytes 663556
  10.1 6.6 %collective-permute-start.1 = (bf16[8,32,128]{2,1,0:T(8,128)(2,1)S(1)}, bf16[8,32,128]{2,1,0:T(8,128)(2,1)S(1)}, u32[]{:S(2)}, u32[]{:S(2)}) collective-permute-start(bf16[8,32,128]{2,1,0:T(8,128)(2,1)S(1)} %get-tuple-element.11), channel_id=1, source_target_pairs={{4,0},{8,4},{12,8},{16,12},{20,16},{24,20},{28,24},{5,1},{9,5},{13... | collective-permute-start | bytes 196616 | tf_op jit(solution)/shard_map/ppermute | solution.py:129
  11.6 6.3 %collective-permute-start = (bf16[8,32,128]{2,1,0:T(8,128)(2,1)S(1)}, bf16[8,32,128]{2,1,0:T(8,128)(2,1)S(1)}, u32[]{:S(2)}, u32[]{:S(2)}) collective-permute-start(bf16[8,32,128]{2,1,0:T(8,128)(2,1)S(1)} %get-tuple-element.12), channel_id=1, source_target_pairs={{0,4},{4,8},{8,12},{12,16},{16,20},{20,24},{24,28},{1,5},{5,9},{9,... | collective-permute-start | bytes 196616 | tf_op jit(solution)/shard_map/ppermute | solution.py:128
  19.7 33.4 %all-to-all-start = ((bf16[4,16,32,128]{3,2,1,0:T(8,128)(2,1)}), bf16[4,16,32,128]{3,2,1,0:T(8,128)(2,1)S(1)}, u32[]{:S(2)}, u32[]{:S(2)}) async-start(bf16[4,16,32,128]{3,2,1,0:T(8,128)(2,1)} %shard_map.85), calls=%async_computation | async-start | bytes 1048576 | tf_op jit(solution)/shard_map/all_to_all | solution.py:150
  53.1 5.5 %copy-start.4 = (bf16[32,27,64]{2,0,1:T(8,128)(2,1)S(1)}, bf16[32,27,64]{2,0,1:T(8,128)(2,1)}, u32[]{:S(2)}) copy-start(bf16[32,27,64]{2,0,1:T(8,128)(2,1)} %param.10) | copy-start | bytes 331780
  53.2 8.5 %collective-permute-start.3 = (bf16[8,32,128]{2,1,0:T(8,128)(2,1)S(1)}, bf16[8,32,128]{2,1,0:T(8,128)(2,1)S(1)}, u32[]{:S(2)}, u32[]{:S(2)}) collective-permute-start(bf16[8,32,128]{2,1,0:T(8,128)(2,1)S(1)} %get-tuple-element.9), channel_id=1, source_target_pairs={{4,0},{8,4},{12,8},{16,12},{20,16},{24,20},{28,24},{5,1},{9,5},{13... | collective-permute-start | bytes 196616 | tf_op jit(solution)/shard_map/ppermute | solution.py:129
  54.7 7.1 %collective-permute-start.2 = (bf16[8,32,128]{2,1,0:T(8,128)(2,1)S(1)}, bf16[8,32,128]{2,1,0:T(8,128)(2,1)S(1)}, u32[]{:S(2)}, u32[]{:S(2)}) collective-permute-start(bf16[8,32,128]{2,1,0:T(8,128)(2,1)S(1)} %get-tuple-element.10), channel_id=1, source_target_pairs={{0,4},{4,8},{8,12},{12,16},{16,20},{20,24},{24,28},{1,5},{5,9},{9,... | collective-permute-start | bytes 196616 | tf_op jit(solution)/shard_map/ppermute | solution.py:128
  59.2 1.2 %copy-start = (bf16[64,64,128]{2,1,0:T(8,128)(2,1)S(1)}, bf16[64,64,128]{2,1,0:T(8,128)(2,1)}, u32[]{:S(2)}) copy-start(bf16[64,64,128]{2,1,0:T(8,128)(2,1)} %all-gather.3.cloned.1.call-done) | copy-start | bytes 3145732
  60.4 1.4 %copy-start.1 = (bf16[64,64,128]{2,1,0:T(8,128)(2,1)S(1)}, bf16[64,64,128]{2,1,0:T(8,128)(2,1)}, u32[]{:S(2)}) copy-start(bf16[64,64,128]{2,1,0:T(8,128)(2,1)} %all-gather.3.cloned.1.call-done) | copy-start | bytes 3145732
  64.5 28.3 %all-to-all-start.1 = ((bf16[64,24,128]{2,1,0:T(8,128)(2,1)}), bf16[64,24,128]{2,1,0:T(8,128)(2,1)S(1)}, u32[]{:S(2)}, u32[]{:S(2)}) async-start(bf16[64,24,128]{2,1,0:T(8,128)(2,1)} %bitcast.24), calls=%async_computation.2 | async-start | bytes 786432 | tf_op jit(solution)/shard_map/all_to_all | solution.py:176
  81.7 28.4 %reduce-scatter.2.cloned.1.call-start = ((), (), s32[]{:S(2)}) async-start(), calls=%async_computation.4 | async-start | bytes 655360 | tf_op jit(solution)/shard_map/reduce_scatter | solution.py:172
  93.7 20.2 %all-to-all-start.2 = ((bf16[64,24,128]{2,1,0:T(8,128)(2,1)}), bf16[64,24,128]{2,1,0:T(8,128)(2,1)S(1)}, u32[]{:S(2)}, u32[]{:S(2)}) async-start(bf16[64,24,128]{2,1,0:T(8,128)(2,1)} %broadcast_in_dim.15), calls=%async_computation.3 | async-start | bytes 786432 | tf_op jit(solution)/shard_map/all_to_all | solution.py:179
Sparse Core Ops, SparseCore 0:
  10.4 48.7 all-gather.2
  85.0 24.9 reduce-scatter.1

commit v2 on v1

v2 whole, which is shorter than its diff:
```python
import jax
import jax.numpy as jnp
from jax import lax
from jax.experimental import pallas as pl
from jax.experimental.pallas import tpu as pltpu
from jax.sharding import PartitionSpec as P

TAPS = 27
ROWS = 32
CELLS = 16
LANES = 128
DEPTH = TAPS * ROWS
CHUNK = 24
PARAMS = pltpu.CompilerParams(vmem_limit_bytes=14 * 1024 * 1024)


def fill_patches(patches, low, own, high):
    lane = lax.broadcasted_iota(jnp.int32, (ROWS, LANES), 1)
    first = lane == 0
    last = lane == LANES - 1
    empty = jnp.zeros((ROWS, LANES), jnp.bfloat16)

    def put(a, b, c, x, y, value):
        row = ((a * 3 + b) * 3 + c) * ROWS
        column = (x * 8 + y) * LANES
        patches[row : row + ROWS, column : column + LANES] = value

    for plane in range(4):
        for y in range(8):
            if plane == 0:
                block = low[y]
            elif plane == 3:
                block = high[y]
            else:
                block = own[(plane - 1) * 8 + y]
            wide = block.astype(jnp.float32)
            after = jnp.where(first, 0.0, pltpu.roll(wide, 1, 1)).astype(jnp.bfloat16)
            before = jnp.where(last, 0.0, pltpu.roll(wide, LANES - 1, 1)).astype(jnp.bfloat16)
            for c, value in enumerate((after, block, before)):
                for a in range(3):
                    x = plane - a
                    if x < 0 or x > 1:
                        continue
                    for b in range(3):
                        target = y + 1 - b
                        if 0 <= target < 8:
                            put(a, b, c, x, target, value)
    for a in range(3):
        for c in range(3):
            for x in range(2):
                put(a, 0, c, x, 0, empty)
                put(a, 2, c, x, 7, empty)


def data_two_kernel(low, own, high, weight, out, patches):
    fill_patches(patches, low, own, high)
    for group in range(4):
        columns = slice(group * 512, group * 512 + 512)
        result = jnp.dot(weight[...], patches[:, columns], preferred_element_type=jnp.float32)
        result = result.astype(jnp.bfloat16)
        for part in range(4):
            for cell in range(4):
                out[part, group * 4 + cell] = result[
                    part * 32 : part * 32 + 32, cell * LANES : cell * LANES + LANES
                ]


def lay_out(fields, me, blocks, start, count):
    own, left, right, far_first, far_second = blocks
    for shift in range(4):
        part = lax.rem(me[0] + shift, 4)
        rows = pl.ds(pl.multiple_of(part * count, count), count)
        for cell in range(CELLS):
            if shift == 2:
                source = far_first[cell] if cell < 8 else far_second[cell - 8]
            else:
                source = (own, right, None, left)[shift][cell]
            fields[rows, cell * LANES : cell * LANES + LANES] = source[start : start + count]


def tap_sums(patches, fields):
    sums = lax.dot_general(
        patches[...], fields[...], (((1,), (1,)), ((), ())), preferred_element_type=jnp.float32
    )
    return jnp.concatenate(
        [sums[(TAPS - 1 - k) * ROWS : (TAPS - k) * ROWS] for k in range(TAPS)], axis=0
    )


def filter_two_kernel(me, low, own, high, b0, b1, b2, b3, b4, out, patches, fields):
    fill_patches(patches, low, own, high)
    lay_out(fields, me, (b0, b1, b2, b3, b4), 0, 32)
    out[...] = tap_sums(patches, fields).astype(jnp.bfloat16)


def pack_kernel(b0, b1, b2, b3, b4, first, second):
    for y in range(8):
        for shift, source in enumerate((b0, b2, b3, b1)):
            first[y, shift * 16 : shift * 16 + 16] = source[y, 32:48]
        for shift, source in enumerate((b0, b2, b4, b1)):
            second[y, shift * 16 : shift * 16 + 16] = source[y if shift == 2 else 8 + y, 32:48]


def filter_one_kernel(
    me, parts, b0, b1, b2, b3, b4, in_low, in_high, filter_two, delta, sums, shifted, fields
):
    lane = lax.broadcasted_iota(jnp.int32, (ROWS, LANES), 1)
    for cell in range(CELLS):
        total = parts[0, cell].astype(jnp.float32)
        for part in range(1, 4):
            total = total + parts[part, cell].astype(jnp.float32)
        total = jnp.where(b0[cell, 0:ROWS].astype(jnp.float32) > 0, total, 0.0)
        block = total.astype(jnp.bfloat16)
        delta[cell] = block
        wide = block.astype(jnp.float32)
        before = jnp.where(lane == LANES - 1, 0.0, pltpu.roll(wide, LANES - 1, 1))
        after = jnp.where(lane == 0, 0.0, pltpu.roll(wide, 1, 1))
        column = cell * LANES
        shifted[0:ROWS, column : column + LANES] = before.astype(jnp.bfloat16)
        shifted[ROWS : 2 * ROWS, column : column + LANES] = block
        shifted[2 * ROWS : 3 * ROWS, column : column + LANES] = after.astype(jnp.bfloat16)
    for shift in range(4):
        part = lax.rem(me[0] + shift, 4)
        rows = pl.ds(pl.multiple_of(part * 16, 16), 16)
        for plane in range(4):
            for y in range(8):
                if plane == 0:
                    value = in_low[y, shift * 16 : shift * 16 + 16]
                elif plane == 3:
                    value = in_high[y, shift * 16 : shift * 16 + 16]
                elif shift == 2:
                    value = (b3, b4)[plane - 1][y, 32:48]
                else:
                    value = (b0, b2, None, b1)[shift][(plane - 1) * 8 + y, 32:48]
                column = (plane * 10 + y + 1) * LANES
                fields[rows, column : column + LANES] = value
    empty = jnp.zeros((64, LANES), jnp.bfloat16)
    for plane in range(4):
        for y in (0, 9):
            column = (plane * 10 + y) * LANES
            fields[:, column : column + LANES] = empty
    taps = []
    for a in range(3):
        for b in range(3):
            total = None
            for x in range(2):
                column = ((x + a) * 10 + b) * LANES
                term = lax.dot_general(
                    shifted[:, x * 1024 : x * 1024 + 1024],
                    fields[:, column : column + 1024],
                    (((1,), (1,)), ((), ())),
                    preferred_element_type=jnp.float32,
                )
                total = term if total is None else total + term
            taps.append(total)
    one = jnp.concatenate(taps, axis=0)
    half = DEPTH // 2
    sums[0:DEPTH] = filter_two[...]
    sums[DEPTH : DEPTH + half] = jnp.concatenate([one[:half], one[half:]], axis=1).astype(jnp.bfloat16)
    sums[DEPTH + half :] = jnp.zeros((64 * CHUNK - DEPTH - half, LANES), jnp.bfloat16)


def data_one_kernel(low, own, high, weight, keep, right, across, left, patches):
    fill_patches(patches, low, own, high)
    for group in range(4):
        columns = slice(group * 512, group * 512 + 512)
        result = jnp.dot(weight[...], patches[:, columns], preferred_element_type=jnp.float32)
        for part, target in enumerate((keep, right, across, left)):
            for cell in range(4):
                target[group * 4 + cell] = result[
                    part * 16 : part * 16 + 16, cell * LANES : cell * LANES + LANES
                ].astype(target.dtype)


def add_kernel(pieces, copies):
    total = pieces[0].astype(jnp.float32)
    for index in range(1, 64):
        total = total + pieces[index].astype(jnp.float32)
    total = total.astype(jnp.bfloat16)
    for index in range(64):
        copies[index] = total


def unpack_kernel(rows, two, one):
    two[...] = rows[0:DEPTH].astype(jnp.float32)
    half = DEPTH // 2
    pairs = rows[DEPTH : DEPTH + half].astype(jnp.float32)
    one[0:half] = pairs[:, 0:64]
    one[half:] = pairs[:, 64:128]


def call(kernel, outs, scratch, flops, arrays, scalars=0):
    memory = pl.BlockSpec(memory_space=pltpu.SMEM)
    return pl.pallas_call(
        kernel,
        out_shape=outs,
        in_specs=[memory] * scalars + [pl.BlockSpec(memory_space=pltpu.VMEM)] * arrays,
        scratch_shapes=scratch,
        compiler_params=PARAMS,
        cost_estimate=pl.CostEstimate(flops=flops, bytes_accessed=1 << 20, transcendentals=0),
    )


def by_rows(field):
    moved = field[0].transpose(1, 2, 0, 3)
    return moved.reshape((CELLS,) + moved.shape[2:])


def neighbours(first, second):
    count = lax.axis_size("space")
    forward = [(i, i + 1) for i in range(count - 1)]
    backward = [(i + 1, i) for i in range(count - 1)]
    low = lax.ppermute(second, "space", forward)
    high = lax.ppermute(first, "space", backward)
    return low, high


def flipped(weights):
    return weights[:, ::-1, :].transpose(2, 1, 0).reshape(weights.shape[2], DEPTH)


def from_this(weights, me, count):
    rows = flipped(weights)
    return lax.dynamic_slice_in_dim(jnp.concatenate([rows, rows], axis=0), me * count, 4 * count, axis=0)


def over_chan(keep, right, across, left):
    ring = lambda step: [(i, (i + step) % 4) for i in range(4)]
    across = lax.ppermute(across, "chan", ring(2))
    right = lax.ppermute(right, "chan", ring(1))
    left = lax.ppermute(left, "chan", ring(3))
    return keep, right, across, left


def shares(count):
    shape = (CELLS, count, LANES)
    return (jax.ShapeDtypeStruct(shape, jnp.float32),) + (jax.ShapeDtypeStruct(shape, jnp.bfloat16),) * 3


def local(inputs, pre_one, pre_two, grad_out, weight_one, weight_two):
    bf16 = jnp.bfloat16
    patches = pltpu.VMEM((DEPTH, CELLS * LANES), bf16)
    delta_two = by_rows(jnp.where(pre_two > 0, grad_out, jnp.zeros_like(grad_out)))
    low_two, high_two = neighbours(delta_two[:8], delta_two[8:])
    hidden = by_rows(jnp.maximum(pre_one, jnp.zeros_like(pre_one)))
    both = jnp.concatenate([hidden, by_rows(inputs)], axis=1)
    to_right = [(i, (i + 1) % 4) for i in range(4)]
    to_left = [(i, (i + 3) % 4) for i in range(4)]
    from_left = lax.ppermute(both, "chan", to_right)
    from_right = lax.ppermute(both, "chan", to_left)
    me = lax.axis_index("chan").astype(jnp.int32)

    partial_two = call(
        data_two_kernel, jax.ShapeDtypeStruct((4, CELLS, 32, LANES), bf16), [patches], 2_500_000_000, 4
    )(low_two, delta_two, high_two, flipped(weight_two))
    partial_two, from_left, from_right = lax.optimization_barrier((partial_two, from_left, from_right))
    parts = lax.all_to_all(partial_two, "chan", 0, 0, tiled=True)

    far_first = lax.ppermute(from_left[:8], "chan", to_right)
    far_second = lax.ppermute(from_right[8:], "chan", to_left)
    blocks = (both, from_left, from_right, far_first, far_second)
    plane = jax.ShapeDtypeStruct((8, 64, LANES), bf16)
    first, second = call(pack_kernel, (plane, plane), [], 8_000_000_000, 5)(*blocks)
    in_low, in_high = neighbours(first, second)
    filter_two = call(
        filter_two_kernel,
        jax.ShapeDtypeStruct((DEPTH, LANES), bf16),
        [patches, pltpu.VMEM((128, CELLS * LANES), bf16)],
        500_000_000,
        8,
        1,
    )(me[None], low_two, delta_two, high_two, *blocks)

    parts, in_low, in_high, filter_two = lax.optimization_barrier((parts, in_low, in_high, filter_two))
    delta_one, sums = call(
        filter_one_kernel,
        (
            jax.ShapeDtypeStruct((CELLS, ROWS, LANES), bf16),
            jax.ShapeDtypeStruct((64 * CHUNK, LANES), bf16),
        ),
        [pltpu.VMEM((3 * ROWS, CELLS * LANES), bf16), pltpu.VMEM((64, 40 * LANES), bf16)],
        500_000_000,
        9,
        1,
    )(me[None], parts, *blocks, in_low, in_high, filter_two)

    every = ("dp", "space")
    pieces = lax.all_to_all(sums.reshape(64, CHUNK, LANES), every, 0, 0, tiled=True)
    low_one, high_one = neighbours(delta_one[:8], delta_one[8:])
    partial_one = call(data_one_kernel, shares(16), [patches], 500_000_000, 4)(
        low_one, delta_one, high_one, from_this(weight_one, me, 16)
    )
    pieces, partial_one = lax.optimization_barrier((pieces, partial_one))
    copies = call(add_kernel, jax.ShapeDtypeStruct((64, CHUNK, LANES), bf16), [], 0, 1)(pieces)
    keep, right, across, left = over_chan(*partial_one)
    input_grad = keep + right.astype(jnp.float32) + across.astype(jnp.float32) + left.astype(jnp.float32)
    input_grad = input_grad.astype(bf16).reshape(2, 8, 16, LANES).transpose(2, 0, 1, 3)[None]
    total = lax.all_to_all(copies, every, 0, 0, tiled=True).reshape(64 * CHUNK, LANES)
    two, one = call(
        unpack_kernel,
        (jax.ShapeDtypeStruct((DEPTH, LANES), jnp.float32), jax.ShapeDtypeStruct((DEPTH, 64), jnp.float32)),
        [],
        0,
        1,
    )(total)
    grad_two = two.reshape(TAPS, ROWS, LANES).transpose(1, 0, 2)
    grad_one = one.reshape(TAPS, ROWS, 64).transpose(1, 0, 2)
    return input_grad, grad_one, grad_two


def solution(mesh):
    field = P("dp", "chan", "space", None, None)
    weight = P("chan", None, None)
    return jax.shard_map(
        local,
        mesh=mesh,
        in_specs=(field, field, field, field, weight, weight),
        out_specs=(field, weight, weight),
        check_vma=False,
    )
```

time: 123 us -> 99.9 us (0.81)
  waiting for transfers between devices: 51.9 us -> 27.2 us
  starting transfers between devices: 41.6 us -> 60.2 us
  between operations: 14.3 us -> 0.86 us
  local copies, waits for them, and re-layouts: 5.87 us -> 1.06 us
  Pallas kernels: 5.9 us -> 8 us
  other arithmetic: 2.95 us -> 1.18 us
    all_to_all x1, waiting for transfers between devices: 25.3 us -> 0.01 us  [local(): parts = lax.all_to_all(partial_two, 'chan', 0, 0, tiled=True)]
    ppermute x4 -> x13, starting transfers between devices: 11.8 us -> 37 us  [the longest x3 16.3 us: neighbours(): low = lax.ppermute(second, 'space', forward)]
    ppermute x4 -> x13, waiting for transfers between devices: 1.11 us -> 25.5 us  [the longest x3 11.5 us: neighbours(): high = lax.ppermute(first, 'space', backward)]
    reduce_scatter x1 -> x0, waiting for transfers between devices: 11.9 us -> none  [local(): lax.psum_scatter(grad, 'chan', scatter_dimension=0, tiled=True)[0]]
    all_to_all x1, waiting for transfers between devices: 10.3 us -> 1.66 us  [local(): lax.all_to_all(sums.reshape(64, CHUNK, LANES), every, 0, 0, tiled=True)]
    all_to_all x1, starting transfers between devices: 17.1 us -> 11.1 us  [local(): lax.all_to_all(sums.reshape(64, CHUNK, LANES), every, 0, 0, tiled=True)]
    all_to_all x1, starting transfers between devices: 7.98 us -> 3.49 us  [local(): parts = lax.all_to_all(partial_two, 'chan', 0, 0, tiled=True)]
    all_to_all x1, starting transfers between devices: 4.53 us -> 8.7 us  [local(): lax.all_to_all(copies, every, 0, 0, tiled=True).reshape(64 * CHUNK, LANES)]
  transfers between devices with their start and end apart: 9 -> 16, of which waited for: 6 -> 10; matrix products, arithmetic and copies ran while one was open for 2% -> 1% of each run, Pallas kernels for 3% -> 4%
where the time goes in v2:
time: 99.9 us; the launch traced here: 98.5 us
  starting transfers between devices  60.2 us (60%)
  waiting for transfers between devices  27.2 us (27%)
  Pallas kernels  8 us (8%)
  other arithmetic  1.18 us (1%)
  local copies, waits for them, and re-layouts  1.06 us (1%)
    ppermute x3, starting transfers between devices, neighbours(): low = lax.ppermute(second, 'space', forward)  16.3 us
    ppermute x3, waiting for transfers between devices, neighbours(): high = lax.ppermute(first, 'space', backward)  11.5 us
    all_to_all x1, starting transfers between devices, local(): lax.all_to_all(sums.reshape(64, CHUNK, LANES), every, 0, 0, tiled=True)  11.1 us
    all_to_all x1, starting transfers between devices, local(): lax.all_to_all(copies, every, 0, 0, tiled=True).reshape(64 * CHUNK, LANES)  8.7 us
    ppermute x3, waiting for transfers between devices, neighbours(): low = lax.ppermute(second, 'space', forward)  4.03 us
    ppermute x3, starting transfers between devices, neighbours(): high = lax.ppermute(first, 'space', backward)  3.88 us
    ppermute x1, starting transfers between devices, over_chan(): left = lax.ppermute(left, 'chan', ring(3))  3.64 us
    ppermute x1, waiting for transfers between devices, over_chan(): across = lax.ppermute(across, 'chan', ring(2))  3.55 us
  transfers between devices with their start and end apart: 16, of which 10 were waited for; matrix products, arithmetic and copies ran while one was open for 1% of the time, Pallas kernels for 4%

profile of v2, /device:TPU:1, one launch (start us, length us, event | category | flops | bytes accessed | tf_op | source)
XLA Modules:
  0.0 98.5 jit_solution(16764116943544884886)
XLA Ops:
  0.6 1.0 %compare_select_fusion = bf16[1,32,2,8,128]{4,1,3,2,0:T(8,128)(2,1)S(1)} fusion(bf16[1,32,2,8,128]{4,3,2,1,0:T(8,128)(2,1)} %param.9, bf16[1,32,2,8,128]{4,3,2,1,0:T(8,128)(2,1)} %param.8), kind=kLoop, calls=%fused_computation | loop fusion | flops 131072 | bytes 393216 | tf_op jit(solution)/shard_map/jit(_where)/select_n | solution.py:243
  1.7 0.0 copy-start.3
  1.7 0.0 copy-start.2
  1.7 4.5 %collective-permute-start = (bf16[8,32,128]{2,1,0:T(8,128)(2,1)S(1)}, bf16[8,32,128]{2,1,0:T(8,128)(2,1)S(1)}, u32[]{:S(2)}, u32[]{:S(2)}) collective-permute-start(bf16[8,32,128]{2,1,0:T(8,128)(2,1)S(1)} %get-tuple-element.50), channel_id=1, source_target_pairs={{0,4},{4,8},{8,12},{12,16},{16,20},{20,24},{24,28},{1,5},{5,9},{9,... | collective-permute-start | bytes 196616 | tf_op jit(solution)/shard_map/ppermute | solution.py:213
  6.2 1.3 %collective-permute-start.1 = (bf16[8,32,128]{2,1,0:T(8,128)(2,1)S(1)}, bf16[8,32,128]{2,1,0:T(8,128)(2,1)S(1)}, u32[]{:S(2)}, u32[]{:S(2)}) collective-permute-start(bf16[8,32,128]{2,1,0:T(8,128)(2,1)S(1)} %get-tuple-element.49), channel_id=1, source_target_pairs={{4,0},{8,4},{12,8},{16,12},{20,16},{24,20},{28,24},{5,1},{9,5},{13... | collective-permute-start | bytes 196616 | tf_op jit(solution)/shard_map/ppermute | solution.py:214
  7.5 0.0 copy-done.3
  7.5 0.0 copy-done.2
  7.6 0.0 copy-start
  7.6 3.1 %collective-permute-start.2 = (bf16[16,48,128]{2,1,0:T(8,128)(2,1)S(1)}, bf16[16,48,128]{2,1,0:T(8,128)(2,1)S(1)}, u32[]{:S(2)}, u32[]{:S(2)}) collective-permute-start(bf16[16,48,128]{2,1,0:T(8,128)(2,1)S(1)} %pad_maximum_fusion.b0), channel_id=1, source_target_pairs={{0,1},{1,2},{2,3},{3,0},{4,5},{5,6},{6,7},{7,4},{8,9},{9,10},{10,1... | collective-permute-start | bytes 589832 | tf_op jit(solution)/shard_map/ppermute | solution.py:249
  10.7 2.2 %collective-permute-start.3 = (bf16[16,48,128]{2,1,0:T(8,128)(2,1)S(1)}, bf16[16,48,128]{2,1,0:T(8,128)(2,1)S(1)}, u32[]{:S(2)}, u32[]{:S(2)}) collective-permute-start(bf16[16,48,128]{2,1,0:T(8,128)(2,1)S(1)} %pad_maximum_fusion.b0), channel_id=1, source_target_pairs={{0,3},{1,0},{2,1},{3,2},{4,7},{5,4},{6,5},{7,6},{8,11},{9,8},{10,9... | collective-permute-start | bytes 589832 | tf_op jit(solution)/shard_map/ppermute | solution.py:250
  12.9 0.0 copy-done
  12.9 0.2 copy.18.weight
  13.1 0.0 collective-permute-done.low
  13.1 0.0 collective-permute-done.1.high
  13.1 1.8 %shard_map.85 = bf16[4,16,32,128]{3,2,1,0:T(8,128)(2,1)} custom-call(bf16[8,32,128]{2,1,0:T(8,128)(2,1)S(1)} %collective-permute-done.low, bf16[16,32,128]{2,1,0:T(8,128)(2,1)S(1)} %bitcast.41, bf16[8,32,128]{2,1,0:T(8,128)(2,1)S(1)} %collective-permute-done.1.high, bf16[128,864]{1,0:T(8,128)(2,1)S(1)} %copy.18.weight), custom_call_target="tpu_custom_call" | custom-call | flops 2500000000 | bytes 1048576 | tf_op jit(solution)/shard_map/pallas_call | solution.py:253
  14.9 2.9 %collective-permute-done.2.b1 = bf16[16,48,128]{2,1,0:T(8,128)(2,1)S(1)} collective-permute-done((bf16[16,48,128]{2,1,0:T(8,128)(2,1)S(1)}, bf16[16,48,128]{2,1,0:T(8,128)(2,1)S(1)}, u32[]{:S(2)}, u32[]{:S(2)}) %collective-permute-start.2) | collective-permute-done | bytes 196640 | tf_op jit(solution)/shard_map/ppermute | solution.py:249
  17.9 1.4 %collective-permute-done.3.b2 = bf16[16,48,128]{2,1,0:T(8,128)(2,1)S(1)} collective-permute-done((bf16[16,48,128]{2,1,0:T(8,128)(2,1)S(1)}, bf16[16,48,128]{2,1,0:T(8,128)(2,1)S(1)}, u32[]{:S(2)}, u32[]{:S(2)}) %collective-permute-start.3) | collective-permute-done | bytes 196640 | tf_op jit(solution)/shard_map/ppermute | solution.py:250
  19.3 2.1 %collective-permute-start.4 = (bf16[8,48,128]{2,1,0:T(8,128)(2,1)S(1)}, bf16[8,48,128]{2,1,0:T(8,128)(2,1)S(1)}, u32[]{:S(2)}, u32[]{:S(2)}) collective-permute-start(bf16[8,48,128]{2,1,0:T(8,128)(2,1)S(1)} %slice.28), channel_id=1, source_target_pairs={{0,1},{1,2},{2,3},{3,0},{4,5},{5,6},{6,7},{7,4},{8,9},{9,10},{10,1... | collective-permute-start | bytes 294920 | tf_op jit(solution)/shard_map/ppermute | solution.py:259
  21.4 1.6 %collective-permute-start.5 = (bf16[8,48,128]{2,1,0:T(8,128)(2,1)S(1)}, bf16[8,48,128]{2,1,0:T(8,128)(2,1)S(1)}, u32[]{:S(2)}, u32[]{:S(2)}) collective-permute-start(bf16[8,48,128]{2,1,0:T(8,128)(2,1)S(1)} %slice.29), channel_id=1, source_target_pairs={{0,3},{1,0},{2,1},{3,2},{4,7},{5,4},{6,5},{7,6},{8,11},{9,8},{10,9... | collective-permute-start | bytes 294920 | tf_op jit(solution)/shard_map/ppermute | solution.py:260
  23.0 3.5 %all-to-all-start = ((bf16[4,16,32,128]{3,2,1,0:T(8,128)(2,1)}), bf16[4,16,32,128]{3,2,1,0:T(8,128)(2,1)S(1)}, u32[]{:S(2)}, u32[]{:S(2)}) async-start(bf16[4,16,32,128]{3,2,1,0:T(8,128)(2,1)} %shard_map.85), calls=%async_computation | async-start | bytes 1048576 | tf_op jit(solution)/shard_map/all_to_all | solution.py:257
  26.5 0.0 collective-permute-done.4.b3
  26.5 0.4 collective-permute-done.5.b4
  26.9 8.5 %collective-permute-start.6 = (bf16[8,64,128]{2,1,0:T(8,128)(2,1)S(1)}, bf16[8,64,128]{2,1,0:T(8,128)(2,1)S(1)}, u32[]{:S(2)}, u32[]{:S(2)}) collective-permute-start(bf16[8,64,128]{2,1,0:T(8,128)(2,1)S(1)} %get-tuple-element.28), channel_id=1, source_target_pairs={{0,4},{4,8},{8,12},{12,16},{16,20},{20,24},{24,28},{1,5},{5,9},{9,... | collective-permute-start | bytes 393224 | tf_op jit(solution)/shard_map/ppermute | solution.py:213
  35.4 1.3 %collective-permute-start.7 = (bf16[8,64,128]{2,1,0:T(8,128)(2,1)S(1)}, bf16[8,64,128]{2,1,0:T(8,128)(2,1)S(1)}, u32[]{:S(2)}, u32[]{:S(2)}) collective-permute-start(bf16[8,64,128]{2,1,0:T(8,128)(2,1)S(1)} %get-tuple-element.29), channel_id=1, source_target_pairs={{4,0},{8,4},{12,8},{16,12},{20,16},{24,20},{28,24},{5,1},{9,5},{13... | collective-permute-start | bytes 393224 | tf_op jit(solution)/shard_map/ppermute | solution.py:214
  36.7 1.3 %shard_map.87.filter_two = bf16[864,128]{1,0:T(8,128)(2,1)S(1)} custom-call(s32[1]{0:T(128)} %bitcast.me, bf16[8,32,128]{2,1,0:T(8,128)(2,1)S(1)} %collective-permute-done.low, bf16[16,32,128]{2,1,0:T(8,128)(2,1)S(1)} %bitcast.42, bf16[8,32,128]{2,1,0:T(8,128)(2,1)S(1)} %collective-permute-done.1.high, bf16[16,48,128]{2,1,0:T(8,128)(2,1)S(1)} %pad_maximum_fusion.b0, ...), custom_call_target="tpu_custom_call" | custom-call | flops 500000000 | bytes 1048576 | tf_op jit(solution)/shard_map/pallas_call | solution.py:265
  38.0 3.4 %collective-permute-done.6.in_low = bf16[8,64,128]{2,1,0:T(8,128)(2,1)S(1)} collective-permute-done((bf16[8,64,128]{2,1,0:T(8,128)(2,1)S(1)}, bf16[8,64,128]{2,1,0:T(8,128)(2,1)S(1)}, u32[]{:S(2)}, u32[]{:S(2)}) %collective-permute-start.6) | collective-permute-done | bytes 131104 | tf_op jit(solution)/shard_map/ppermute | solution.py:213
  41.4 8.2 %collective-permute-done.7.in_high = bf16[8,64,128]{2,1,0:T(8,128)(2,1)S(1)} collective-permute-done((bf16[8,64,128]{2,1,0:T(8,128)(2,1)S(1)}, bf16[8,64,128]{2,1,0:T(8,128)(2,1)S(1)}, u32[]{:S(2)}, u32[]{:S(2)}) %collective-permute-start.7) | collective-permute-done | bytes 131104 | tf_op jit(solution)/shard_map/ppermute | solution.py:214
  49.6 0.0 all-to-all-done.parts
  49.6 2.0 %shard_map.88 = (bf16[16,32,128]{2,1,0:T(8,128)(2,1)S(1)}, bf16[1536,128]{1,0:T(8,128)(2,1)}) custom-call(s32[1]{0:T(128)} %bitcast.me, bf16[4,16,32,128]{3,2,1,0:T(8,128)(2,1)S(1)} %all-to-all-done.parts, bf16[16,48,128]{2,1,0:T(8,128)(2,1)S(1)} %pad_maximum_fusion.b0, bf16[16,48,128]{2,1,0:T(8,128)(2,1)S(1)} %collective-permute-done.2.b1, ...), custom_call_target="tpu_custom_call" | custom-call | flops 500000000 | bytes 1048576 | tf_op jit(solution)/shard_map/pallas_call | solution.py:275
  51.6 0.0 copy-start.1
  51.7 11.1 %all-to-all-start.1 = ((bf16[64,24,128]{2,1,0:T(8,128)(2,1)}), bf16[64,24,128]{2,1,0:T(8,128)(2,1)S(1)}, u32[]{:S(2)}, u32[]{:S(2)}) async-start(bf16[64,24,128]{2,1,0:T(8,128)(2,1)} %bitcast.16), calls=%async_computation.1 | async-start | bytes 786432 | tf_op jit(solution)/shard_map/all_to_all | solution.py:288
  62.7 0.0 copy-done.1
  62.7 0.1 copy.21
  62.9 3.3 %collective-permute-start.8 = (bf16[8,32,128]{2,1,0:T(8,128)(2,1)S(1)}, bf16[8,32,128]{2,1,0:T(8,128)(2,1)S(1)}, u32[]{:S(2)}, u32[]{:S(2)}) collective-permute-start(bf16[8,32,128]{2,1,0:T(8,128)(2,1)S(1)} %get-tuple-element.48), channel_id=1, source_target_pairs={{0,4},{4,8},{8,12},{12,16},{16,20},{20,24},{24,28},{1,5},{5,9},{9,... | collective-permute-start | bytes 196616 | tf_op jit(solution)/shard_map/ppermute | solution.py:213
  66.2 1.3 %collective-permute-start.9 = (bf16[8,32,128]{2,1,0:T(8,128)(2,1)S(1)}, bf16[8,32,128]{2,1,0:T(8,128)(2,1)S(1)}, u32[]{:S(2)}, u32[]{:S(2)}) collective-permute-start(bf16[8,32,128]{2,1,0:T(8,128)(2,1)S(1)} %get-tuple-element.47), channel_id=1, source_target_pairs={{4,0},{8,4},{12,8},{16,12},{20,16},{24,20},{28,24},{5,1},{9,5},{13... | collective-permute-start | bytes 196616 | tf_op jit(solution)/shard_map/ppermute | solution.py:214
  67.5 0.1 fusion.weight
  67.6 0.7 collective-permute-done.8.low
  68.2 3.3 %collective-permute-done.9.high = bf16[8,32,128]{2,1,0:T(8,128)(2,1)S(1)} collective-permute-done((bf16[8,32,128]{2,1,0:T(8,128)(2,1)S(1)}, bf16[8,32,128]{2,1,0:T(8,128)(2,1)S(1)}, u32[]{:S(2)}, u32[]{:S(2)}) %collective-permute-start.9) | collective-permute-done | bytes 65568 | tf_op jit(solution)/shard_map/ppermute | solution.py:214
  71.5 1.0 %shard_map.89 = (f32[16,16,128]{2,1,0:T(8,128)S(1)}, bf16[16,16,128]{2,1,0:T(8,128)(2,1)S(1)}, bf16[16,16,128]{2,1,0:T(8,128)(2,1)S(1)}, bf16[16,16,128]{2,1,0:T(8,128)(2,1)S(1)}) custom-call(bf16[8,32,128]{2,1,0:T(8,128)(2,1)S(1)} %collective-permute-done.8.low, bf16[16,32,128]{2,1,0:T(8,128)(2,1)S(1)} %get-tuple-element.35.own, ...), custom_call_target="tpu_custom_call" | custom-call | flops 500000000 | bytes 1048576 | tf_op jit(solution)/shard_map/pallas_call | solution.py:290
  72.5 1.7 %all-to-all-done.1.pieces = bf16[64,24,128]{2,1,0:T(8,128)(2,1)S(1)} async-done(((bf16[64,24,128]{2,1,0:T(8,128)(2,1)}), bf16[64,24,128]{2,1,0:T(8,128)(2,1)S(1)}, u32[]{:S(2)}, u32[]{:S(2)}) %all-to-all-start.1) | async-done | bytes 393248 | tf_op jit(solution)/shard_map/all_to_all | solution.py:288
  74.2 0.8 shard_map.90
  75.0 8.7 %all-to-all-start.2 = ((bf16[64,24,128]{2,1,0:T(8,128)(2,1)}), bf16[64,24,128]{2,1,0:T(8,128)(2,1)S(1)}, u32[]{:S(2)}, u32[]{:S(2)}) async-start(bf16[64,24,128]{2,1,0:T(8,128)(2,1)} %shard_map.90), calls=%async_computation.2 | async-start | bytes 786432 | tf_op jit(solution)/shard_map/all_to_all | solution.py:298
  83.7 3.6 %collective-permute-start.12 = (bf16[16,16,128]{2,1,0:T(8,128)(2,1)S(1)}, bf16[16,16,128]{2,1,0:T(8,128)(2,1)S(1)}, u32[]{:S(2)}, u32[]{:S(2)}) collective-permute-start(bf16[16,16,128]{2,1,0:T(8,128)(2,1)S(1)} %get-tuple-element.43), channel_id=1, source_target_pairs={{0,3},{1,0},{2,1},{3,2},{4,7},{5,4},{6,5},{7,6},{8,11},{9,8},{10,9... | collective-permute-start | bytes 196616 | tf_op jit(solution)/shard_map/ppermute | solution.py:231
  87.4 2.1 %collective-permute-start.11 = (bf16[16,16,128]{2,1,0:T(8,128)(2,1)S(1)}, bf16[16,16,128]{2,1,0:T(8,128)(2,1)S(1)}, u32[]{:S(2)}, u32[]{:S(2)}) collective-permute-start(bf16[16,16,128]{2,1,0:T(8,128)(2,1)S(1)} %get-tuple-element.42), channel_id=1, source_target_pairs={{0,2},{1,3},{2,0},{3,1},{4,6},{5,7},{6,4},{7,5},{8,10},{9,11},{10,... | collective-permute-start | bytes 196616 | tf_op jit(solution)/shard_map/ppermute | solution.py:229
  89.4 2.1 %collective-permute-start.10 = (bf16[16,16,128]{2,1,0:T(8,128)(2,1)S(1)}, bf16[16,16,128]{2,1,0:T(8,128)(2,1)S(1)}, u32[]{:S(2)}, u32[]{:S(2)}) collective-permute-start(bf16[16,16,128]{2,1,0:T(8,128)(2,1)S(1)} %get-tuple-element.41), channel_id=1, source_target_pairs={{0,1},{1,2},{2,3},{3,0},{4,5},{5,6},{6,7},{7,4},{8,9},{9,10},{10,1... | collective-permute-start | bytes 196616 | tf_op jit(solution)/shard_map/ppermute | solution.py:230
  91.5 0.0 collective-permute-done.12
  91.5 3.6 %collective-permute-done.11 = bf16[16,16,128]{2,1,0:T(8,128)(2,1)S(1)} collective-permute-done((bf16[16,16,128]{2,1,0:T(8,128)(2,1)S(1)}, bf16[16,16,128]{2,1,0:T(8,128)(2,1)S(1)}, u32[]{:S(2)}, u32[]{:S(2)}) %collective-permute-start.11) | collective-permute-done | bytes 65568 | tf_op jit(solution)/shard_map/ppermute | solution.py:229
  95.1 1.8 %collective-permute-done.10 = bf16[16,16,128]{2,1,0:T(8,128)(2,1)S(1)} collective-permute-done((bf16[16,16,128]{2,1,0:T(8,128)(2,1)S(1)}, bf16[16,16,128]{2,1,0:T(8,128)(2,1)S(1)}, u32[]{:S(2)}, u32[]{:S(2)}) %collective-permute-start.10) | collective-permute-done | bytes 65568 | tf_op jit(solution)/shard_map/ppermute | solution.py:230
  96.9 0.6 copy.28
  97.6 0.0 all-to-all-done.2
  97.6 1.0 shard_map.91
  (11 shorter events, 0.2 us)
Async XLA Ops:
  1.7 5.9 %copy-start.3 = (bf16[1,16,2,8,128]{4,3,2,1,0:T(8,128)(2,1)S(1)}, bf16[1,16,2,8,128]{4,3,2,1,0:T(8,128)(2,1)}, u32[]{:S(2)}) copy-start(bf16[1,16,2,8,128]{4,3,2,1,0:T(8,128)(2,1)} %param.6) | copy-start | bytes 196612
  1.7 5.9 %copy-start.2 = (bf16[1,32,2,8,128]{4,3,2,1,0:T(8,128)(2,1)S(1)}, bf16[1,32,2,8,128]{4,3,2,1,0:T(8,128)(2,1)}, u32[]{:S(2)}) copy-start(bf16[1,32,2,8,128]{4,3,2,1,0:T(8,128)(2,1)} %param.7) | copy-start | bytes 393220
  1.7 11.4 %collective-permute-start = (bf16[8,32,128]{2,1,0:T(8,128)(2,1)S(1)}, bf16[8,32,128]{2,1,0:T(8,128)(2,1)S(1)}, u32[]{:S(2)}, u32[]{:S(2)}) collective-permute-start(bf16[8,32,128]{2,1,0:T(8,128)(2,1)S(1)} %get-tuple-element.50), channel_id=1, source_target_pairs={{0,4},{4,8},{8,12},{12,16},{16,20},{20,24},{24,28},{1,5},{5,9},{9,... | collective-permute-start | bytes 196616 | tf_op jit(solution)/shard_map/ppermute | solution.py:213
  6.2 6.9 %collective-permute-start.1 = (bf16[8,32,128]{2,1,0:T(8,128)(2,1)S(1)}, bf16[8,32,128]{2,1,0:T(8,128)(2,1)S(1)}, u32[]{:S(2)}, u32[]{:S(2)}) collective-permute-start(bf16[8,32,128]{2,1,0:T(8,128)(2,1)S(1)} %get-tuple-element.49), channel_id=1, source_target_pairs={{4,0},{8,4},{12,8},{16,12},{20,16},{24,20},{28,24},{5,1},{9,5},{13... | collective-permute-start | bytes 196616 | tf_op jit(solution)/shard_map/ppermute | solution.py:214
  7.6 5.3 %copy-start = (bf16[32,27,128]{2,0,1:T(8,128)(2,1)S(1)}, bf16[32,27,128]{2,0,1:T(8,128)(2,1)}, u32[]{:S(2)}) copy-start(bf16[32,27,128]{2,0,1:T(8,128)(2,1)} %param.11) | copy-start | bytes 663556
  7.6 10.2 %collective-permute-start.2 = (bf16[16,48,128]{2,1,0:T(8,128)(2,1)S(1)}, bf16[16,48,128]{2,1,0:T(8,128)(2,1)S(1)}, u32[]{:S(2)}, u32[]{:S(2)}) collective-permute-start(bf16[16,48,128]{2,1,0:T(8,128)(2,1)S(1)} %pad_maximum_fusion.b0), channel_id=1, source_target_pairs={{0,1},{1,2},{2,3},{3,0},{4,5},{5,6},{6,7},{7,4},{8,9},{9,10},{10,1... | collective-permute-start | bytes 589832 | tf_op jit(solution)/shard_map/ppermute | solution.py:249
  10.7 8.5 %collective-permute-start.3 = (bf16[16,48,128]{2,1,0:T(8,128)(2,1)S(1)}, bf16[16,48,128]{2,1,0:T(8,128)(2,1)S(1)}, u32[]{:S(2)}, u32[]{:S(2)}) collective-permute-start(bf16[16,48,128]{2,1,0:T(8,128)(2,1)S(1)} %pad_maximum_fusion.b0), channel_id=1, source_target_pairs={{0,3},{1,0},{2,1},{3,2},{4,7},{5,4},{6,5},{7,6},{8,11},{9,8},{10,9... | collective-permute-start | bytes 589832 | tf_op jit(solution)/shard_map/ppermute | solution.py:250
  19.3 7.2 %collective-permute-start.4 = (bf16[8,48,128]{2,1,0:T(8,128)(2,1)S(1)}, bf16[8,48,128]{2,1,0:T(8,128)(2,1)S(1)}, u32[]{:S(2)}, u32[]{:S(2)}) collective-permute-start(bf16[8,48,128]{2,1,0:T(8,128)(2,1)S(1)} %slice.28), channel_id=1, source_target_pairs={{0,1},{1,2},{2,3},{3,0},{4,5},{5,6},{6,7},{7,4},{8,9},{9,10},{10,1... | collective-permute-start | bytes 294920 | tf_op jit(solution)/shard_map/ppermute | solution.py:259
  21.4 5.5 %collective-permute-start.5 = (bf16[8,48,128]{2,1,0:T(8,128)(2,1)S(1)}, bf16[8,48,128]{2,1,0:T(8,128)(2,1)S(1)}, u32[]{:S(2)}, u32[]{:S(2)}) collective-permute-start(bf16[8,48,128]{2,1,0:T(8,128)(2,1)S(1)} %slice.29), channel_id=1, source_target_pairs={{0,3},{1,0},{2,1},{3,2},{4,7},{5,4},{6,5},{7,6},{8,11},{9,8},{10,9... | collective-permute-start | bytes 294920 | tf_op jit(solution)/shard_map/ppermute | solution.py:260
  23.0 26.6 %all-to-all-start = ((bf16[4,16,32,128]{3,2,1,0:T(8,128)(2,1)}), bf16[4,16,32,128]{3,2,1,0:T(8,128)(2,1)S(1)}, u32[]{:S(2)}, u32[]{:S(2)}) async-start(bf16[4,16,32,128]{3,2,1,0:T(8,128)(2,1)} %shard_map.85), calls=%async_computation | async-start | bytes 1048576 | tf_op jit(solution)/shard_map/all_to_all | solution.py:257
  26.9 14.5 %collective-permute-start.6 = (bf16[8,64,128]{2,1,0:T(8,128)(2,1)S(1)}, bf16[8,64,128]{2,1,0:T(8,128)(2,1)S(1)}, u32[]{:S(2)}, u32[]{:S(2)}) collective-permute-start(bf16[8,64,128]{2,1,0:T(8,128)(2,1)S(1)} %get-tuple-element.28), channel_id=1, source_target_pairs={{0,4},{4,8},{8,12},{12,16},{16,20},{20,24},{24,28},{1,5},{5,9},{9,... | collective-permute-start | bytes 393224 | tf_op jit(solution)/shard_map/ppermute | solution.py:213
  35.4 14.2 %collective-permute-start.7 = (bf16[8,64,128]{2,1,0:T(8,128)(2,1)S(1)}, bf16[8,64,128]{2,1,0:T(8,128)(2,1)S(1)}, u32[]{:S(2)}, u32[]{:S(2)}) collective-permute-start(bf16[8,64,128]{2,1,0:T(8,128)(2,1)S(1)} %get-tuple-element.29), channel_id=1, source_target_pairs={{4,0},{8,4},{12,8},{16,12},{20,16},{24,20},{28,24},{5,1},{9,5},{13... | collective-permute-start | bytes 393224 | tf_op jit(solution)/shard_map/ppermute | solution.py:214
  51.6 11.1 %copy-start.1 = (bf16[32,27,64]{2,0,1:T(8,128)(2,1)S(1)}, bf16[32,27,64]{2,0,1:T(8,128)(2,1)}, u32[]{:S(2)}) copy-start(bf16[32,27,64]{2,0,1:T(8,128)(2,1)} %param.10) | copy-start | bytes 331780
  51.7 22.5 %all-to-all-start.1 = ((bf16[64,24,128]{2,1,0:T(8,128)(2,1)}), bf16[64,24,128]{2,1,0:T(8,128)(2,1)S(1)}, u32[]{:S(2)}, u32[]{:S(2)}) async-start(bf16[64,24,128]{2,1,0:T(8,128)(2,1)} %bitcast.16), calls=%async_computation.1 | async-start | bytes 786432 | tf_op jit(solution)/shard_map/all_to_all | solution.py:288
  62.9 5.3 %collective-permute-start.8 = (bf16[8,32,128]{2,1,0:T(8,128)(2,1)S(1)}, bf16[8,32,128]{2,1,0:T(8,128)(2,1)S(1)}, u32[]{:S(2)}, u32[]{:S(2)}) collective-permute-start(bf16[8,32,128]{2,1,0:T(8,128)(2,1)S(1)} %get-tuple-element.48), channel_id=1, source_target_pairs={{0,4},{4,8},{8,12},{12,16},{16,20},{20,24},{24,28},{1,5},{5,9},{9,... | collective-permute-start | bytes 196616 | tf_op jit(solution)/shard_map/ppermute | solution.py:213
  66.2 5.3 %collective-permute-start.9 = (bf16[8,32,128]{2,1,0:T(8,128)(2,1)S(1)}, bf16[8,32,128]{2,1,0:T(8,128)(2,1)S(1)}, u32[]{:S(2)}, u32[]{:S(2)}) collective-permute-start(bf16[8,32,128]{2,1,0:T(8,128)(2,1)S(1)} %get-tuple-element.47), channel_id=1, source_target_pairs={{4,0},{8,4},{12,8},{16,12},{20,16},{24,20},{28,24},{5,1},{9,5},{13... | collective-permute-start | bytes 196616 | tf_op jit(solution)/shard_map/ppermute | solution.py:214
  75.0 22.5 %all-to-all-start.2 = ((bf16[64,24,128]{2,1,0:T(8,128)(2,1)}), bf16[64,24,128]{2,1,0:T(8,128)(2,1)S(1)}, u32[]{:S(2)}, u32[]{:S(2)}) async-start(bf16[64,24,128]{2,1,0:T(8,128)(2,1)} %shard_map.90), calls=%async_computation.2 | async-start | bytes 786432 | tf_op jit(solution)/shard_map/all_to_all | solution.py:298
  83.7 7.8 %collective-permute-start.12 = (bf16[16,16,128]{2,1,0:T(8,128)(2,1)S(1)}, bf16[16,16,128]{2,1,0:T(8,128)(2,1)S(1)}, u32[]{:S(2)}, u32[]{:S(2)}) collective-permute-start(bf16[16,16,128]{2,1,0:T(8,128)(2,1)S(1)} %get-tuple-element.43), channel_id=1, source_target_pairs={{0,3},{1,0},{2,1},{3,2},{4,7},{5,4},{6,5},{7,6},{8,11},{9,8},{10,9... | collective-permute-start | bytes 196616 | tf_op jit(solution)/shard_map/ppermute | solution.py:231
  87.4 7.7 %collective-permute-start.11 = (bf16[16,16,128]{2,1,0:T(8,128)(2,1)S(1)}, bf16[16,16,128]{2,1,0:T(8,128)(2,1)S(1)}, u32[]{:S(2)}, u32[]{:S(2)}) collective-permute-start(bf16[16,16,128]{2,1,0:T(8,128)(2,1)S(1)} %get-tuple-element.42), channel_id=1, source_target_pairs={{0,2},{1,3},{2,0},{3,1},{4,6},{5,7},{6,4},{7,5},{8,10},{9,11},{10,... | collective-permute-start | bytes 196616 | tf_op jit(solution)/shard_map/ppermute | solution.py:229
  89.4 7.4 %collective-permute-start.10 = (bf16[16,16,128]{2,1,0:T(8,128)(2,1)S(1)}, bf16[16,16,128]{2,1,0:T(8,128)(2,1)S(1)}, u32[]{:S(2)}, u32[]{:S(2)}) collective-permute-start(bf16[16,16,128]{2,1,0:T(8,128)(2,1)S(1)} %get-tuple-element.41), channel_id=1, source_target_pairs={{0,1},{1,2},{2,3},{3,0},{4,5},{5,6},{6,7},{7,4},{8,9},{9,10},{10,1... | collective-permute-start | bytes 196616 | tf_op jit(solution)/shard_map/ppermute | solution.py:230

commit v3 on v2

--- a/solution.py
+++ b/solution.py
@@ -93,67 +93,15 @@
     out[...] = tap_sums(patches, fields).astype(jnp.bfloat16)
 
 
-def pack_kernel(b0, b1, b2, b3, b4, first, second):
-    for y in range(8):
-        for shift, source in enumerate((b0, b2, b3, b1)):
-            first[y, shift * 16 : shift * 16 + 16] = source[y, 32:48]
-        for shift, source in enumerate((b0, b2, b4, b1)):
-            second[y, shift * 16 : shift * 16 + 16] = source[y if shift == 2 else 8 + y, 32:48]
-
-
-def filter_one_kernel(
-    me, parts, b0, b1, b2, b3, b4, in_low, in_high, filter_two, delta, sums, shifted, fields
-):
-    lane = lax.broadcasted_iota(jnp.int32, (ROWS, LANES), 1)
-    for cell in range(CELLS):
-        total = parts[0, cell].astype(jnp.float32)
-        for part in range(1, 4):
-            total = total + parts[part, cell].astype(jnp.float32)
-        total = jnp.where(b0[cell, 0:ROWS].astype(jnp.float32) > 0, total, 0.0)
-        block = total.astype(jnp.bfloat16)
-        delta[cell] = block
-        wide = block.astype(jnp.float32)
-        before = jnp.where(lane == LANES - 1, 0.0, pltpu.roll(wide, LANES - 1, 1))
-        after = jnp.where(lane == 0, 0.0, pltpu.roll(wide, 1, 1))
-        column = cell * LANES
-        shifted[0:ROWS, column : column + LANES] = before.astype(jnp.bfloat16)
-        shifted[ROWS : 2 * ROWS, column : column + LANES] = block
-        shifted[2 * ROWS : 3 * ROWS, column : column + LANES] = after.astype(jnp.bfloat16)
-    for shift in range(4):
-        part = lax.rem(me[0] + shift, 4)
-        rows = pl.ds(pl.multiple_of(part * 16, 16), 16)
-        for plane in range(4):
-            for y in range(8):
-                if plane == 0:
-                    value = in_low[y, shift * 16 : shift * 16 + 16]
-                elif plane == 3:
-                    value = in_high[y, shift * 16 : shift * 16 + 16]
-                elif shift == 2:
-                    value = (b3, b4)[plane - 1][y, 32:48]
-                else:
-                    value = (b0, b2, None, b1)[shift][(plane - 1) * 8 + y, 32:48]
-                column = (plane * 10 + y + 1) * LANES
-                fields[rows, column : column + LANES] = value
-    empty = jnp.zeros((64, LANES), jnp.bfloat16)
-    for plane in range(4):
-        for y in (0, 9):
-            column = (plane * 10 + y) * LANES
-            fields[:, column : column + LANES] = empty
-    taps = []
-    for a in range(3):
-        for b in range(3):
-            total = None
-            for x in range(2):
-                column = ((x + a) * 10 + b) * LANES
-                term = lax.dot_general(
-                    shifted[:, x * 1024 : x * 1024 + 1024],
-                    fields[:, column : column + 1024],
-                    (((1,), (1,)), ((), ())),
-                    preferred_element_type=jnp.float32,
-                )
-                total = term if total is None else total + term
-            taps.append(total)
-    one = jnp.concatenate(taps, axis=0)
+def pass_kernel(from_left, from_right, first, second):
+    first[...] = from_left[0:8]
+    second[...] = from_right[8:16]
+
+
+def filter_one_kernel(me, low, own, high, b0, b1, b2, b3, b4, filter_two, sums, patches, fields):
+    fill_patches(patches, low, own, high)
+    lay_out(fields, me, (b0, b1, b2, b3, b4), 32, 16)
+    one = tap_sums(patches, fields)
     half = DEPTH // 2
     sums[0:DEPTH] = filter_two[...]
     sums[DEPTH : DEPTH + half] = jnp.concatenate([one[:half], one[half:]], axis=1).astype(jnp.bfloat16)
@@ -222,14 +170,6 @@
 def from_this(weights, me, count):
     rows = flipped(weights)
     return lax.dynamic_slice_in_dim(jnp.concatenate([rows, rows], axis=0), me * count, 4 * count, axis=0)
-
-
-def over_chan(keep, right, across, left):
-    ring = lambda step: [(i, (i + step) % 4) for i in range(4)]
-    across = lax.ppermute(across, "chan", ring(2))
-    right = lax.ppermute(right, "chan", ring(1))
-    left = lax.ppermute(left, "chan", ring(3))
-    return keep, right, across, left
 
 
 def shares(count):
@@ -253,15 +193,18 @@
     partial_two = call(
         data_two_kernel, jax.ShapeDtypeStruct((4, CELLS, 32, LANES), bf16), [patches], 2_500_000_000, 4
     )(low_two, delta_two, high_two, flipped(weight_two))
-    partial_two, from_left, from_right = lax.optimization_barrier((partial_two, from_left, from_right))
     parts = lax.all_to_all(partial_two, "chan", 0, 0, tiled=True)
 
-    far_first = lax.ppermute(from_left[:8], "chan", to_right)
-    far_second = lax.ppermute(from_right[8:], "chan", to_left)
+    halves = call(pass_kernel, (jax.ShapeDtypeStruct((8, 48, LANES), bf16),) * 2, [], 11_000_000_000, 2)(
+        from_left, from_right
+    )
+    far_first = lax.ppermute(halves[0], "chan", to_right)
+    far_second = lax.ppermute(halves[1], "chan", to_left)
     blocks = (both, from_left, from_right, far_first, far_second)
-    plane = jax.ShapeDtypeStruct((8, 64, LANES), bf16)
-    first, second = call(pack_kernel, (plane, plane), [], 8_000_000_000, 5)(*blocks)
-    in_low, in_high = neighbours(first, second)
+
+    hidden_grad = jnp.sum(parts.astype(jnp.float32), axis=0)
+    delta_one = jnp.where(hidden > 0, hidden_grad, jnp.zeros_like(hidden_grad)).astype(bf16)
+    low_one, high_one = neighbours(delta_one[:8], delta_one[8:])
     filter_two = call(
         filter_two_kernel,
         jax.ShapeDtypeStruct((DEPTH, LANES), bf16),
@@ -271,28 +214,27 @@
         1,
     )(me[None], low_two, delta_two, high_two, *blocks)
 
-    parts, in_low, in_high, filter_two = lax.optimization_barrier((parts, in_low, in_high, filter_two))
-    delta_one, sums = call(
+    sums = call(
         filter_one_kernel,
-        (
-            jax.ShapeDtypeStruct((CELLS, ROWS, LANES), bf16),
-            jax.ShapeDtypeStruct((64 * CHUNK, LANES), bf16),
-        ),
-        [pltpu.VMEM((3 * ROWS, CELLS * LANES), bf16), pltpu.VMEM((64, 40 * LANES), bf16)],
+        jax.ShapeDtypeStruct((64 * CHUNK, LANES), bf16),
+        [patches, pltpu.VMEM((64, CELLS * LANES), bf16)],
         500_000_000,
         9,
         1,
-    )(me[None], parts, *blocks, in_low, in_high, filter_two)
+    )(me[None], low_one, delta_one, high_one, *blocks, filter_two)
 
     every = ("dp", "space")
+    sums, low_one, high_one = lax.optimization_barrier((sums, low_one, high_one))
     pieces = lax.all_to_all(sums.reshape(64, CHUNK, LANES), every, 0, 0, tiled=True)
-    low_one, high_one = neighbours(delta_one[:8], delta_one[8:])
+    pieces, low_one, high_one = lax.optimization_barrier((pieces, low_one, high_one))
+    copies = call(add_kernel, jax.ShapeDtypeStruct((64, CHUNK, LANES), bf16), [], 0, 1)(pieces)
     partial_one = call(data_one_kernel, shares(16), [patches], 500_000_000, 4)(
         low_one, delta_one, high_one, from_this(weight_one, me, 16)
     )
-    pieces, partial_one = lax.optimization_barrier((pieces, partial_one))
-    copies = call(add_kernel, jax.ShapeDtypeStruct((64, CHUNK, LANES), bf16), [], 0, 1)(pieces)
-    keep, right, across, left = over_chan(*partial_one)
+    keep, right, across, left = partial_one
+    across = lax.ppermute(across, "chan", [(i, (i + 2) % 4) for i in range(4)])
+    right = lax.ppermute(right, "chan", to_right)
+    left = lax.ppermute(left, "chan", to_left)
     input_grad = keep + right.astype(jnp.float32) + across.astype(jnp.float32) + left.astype(jnp.float32)
     input_grad = input_grad.astype(bf16).reshape(2, 8, 16, LANES).transpose(2, 0, 1, 3)[None]
     total = lax.all_to_all(copies, every, 0, 0, tiled=True).reshape(64 * CHUNK, LANES)

time: 99.9 us -> 95.5 us (0.956)
  blocking collectives: 0 us -> 31.4 us
  starting transfers between devices: 60.2 us -> 35.2 us
  waiting for transfers between devices: 27.2 us -> 17.6 us
    all_to_all x0 -> x1, blocking collectives: none -> 31.4 us  [local(): lax.all_to_all(sums.reshape(64, CHUNK, LANES), every, 0, 0, tiled=True)]
    all_to_all x1 -> x0, starting transfers between devices: 11.1 us -> none  [local(): lax.all_to_all(sums.reshape(64, CHUNK, LANES), every, 0, 0, tiled=True)]
    ppermute x3 -> x2, waiting for transfers between devices: 11.5 us -> 4.27 us  [neighbours(): high = lax.ppermute(first, 'space', backward)]
    ppermute x3 -> x2, starting transfers between devices: 16.3 us -> 9.64 us  [neighbours(): low = lax.ppermute(second, 'space', forward)]
    all_to_all x1, waiting for transfers between devices: 0.01 us -> 5.85 us  [local(): parts = lax.all_to_all(partial_two, 'chan', 0, 0, tiled=True)]
    ppermute x5, starting transfers between devices: 11.5 us -> 7.26 us  [the longest x1 3.44 us: local(): across = lax.ppermute(across, 'chan', [(i, (i + 2) % 4) for i in range(4)])]
    all_to_all x1, starting transfers between devices: 8.7 us -> 4.66 us  [local(): lax.all_to_all(copies, every, 0, 0, tiled=True).reshape(64 * CHUNK, LANES)]
    ppermute x3 -> x2, waiting for transfers between devices: 4.03 us -> 0.01 us  [neighbours(): low = lax.ppermute(second, 'space', forward)]
  transfers between devices with their start and end apart: 16 -> 13, of which waited for: 10 -> 6; matrix products, arithmetic and copies ran while one was open for 1% -> 1% of each run, Pallas kernels for 4% -> 4%
where the time goes in v3:
time: 95.5 us; the launch traced here: 94.7 us
  starting transfers between devices  35.2 us (37%)
  blocking collectives  31.4 us (33%)
  waiting for transfers between devices  17.6 us (18%)
  Pallas kernels  7.23 us (8%)
  other arithmetic  1.3 us (1%)
  local copies, waits for them, and re-layouts  1.05 us (1%)
    all_to_all x1, blocking collectives, local(): lax.all_to_all(sums.reshape(64, CHUNK, LANES), every, 0, 0, tiled=True)  31.4 us
    ppermute x2, starting transfers between devices, neighbours(): low = lax.ppermute(second, 'space', forward)  9.64 us
    all_to_all x1, waiting for transfers between devices, local(): parts = lax.all_to_all(partial_two, 'chan', 0, 0, tiled=True)  5.85 us
    all_to_all x1, starting transfers between devices, local(): parts = lax.all_to_all(partial_two, 'chan', 0, 0, tiled=True)  5.65 us
    all_to_all x1, starting transfers between devices, local(): lax.all_to_all(copies, every, 0, 0, tiled=True).reshape(64 * CHUNK, LANES)  4.66 us
    ppermute x2, waiting for transfers between devices, neighbours(): high = lax.ppermute(first, 'space', backward)  4.27 us
    ppermute x1, waiting for transfers between devices, local(): across = lax.ppermute(across, 'chan', [(i, (i + 2) % 4) for i in range(4)])  3.97 us
    ppermute x1, starting transfers between devices, local(): across = lax.ppermute(across, 'chan', [(i, (i + 2) % 4) for i in range(4)])  3.44 us
  transfers between devices with their start and end apart: 13, of which 6 were waited for; matrix products, arithmetic and copies ran while one was open for 1% of the time, Pallas kernels for 4%

profile of v3, /device:TPU:1, one launch (start us, length us, event | category | flops | bytes accessed | tf_op | source)
XLA Modules:
  0.0 94.7 jit_solution(17679820553544502135)
XLA Ops:
  0.6 1.0 %compare_select_fusion = bf16[1,32,2,8,128]{4,1,3,2,0:T(8,128)(2,1)S(1)} fusion(bf16[1,32,2,8,128]{4,3,2,1,0:T(8,128)(2,1)} %param.9, bf16[1,32,2,8,128]{4,3,2,1,0:T(8,128)(2,1)} %param.8), kind=kLoop, calls=%fused_computation.2 | loop fusion | flops 131072 | bytes 393216 | tf_op jit(solution)/shard_map/jit(_where)/select_n | solution.py:183
  1.7 0.0 copy-start.2
  1.7 4.5 %collective-permute-start = (bf16[8,32,128]{2,1,0:T(8,128)(2,1)S(1)}, bf16[8,32,128]{2,1,0:T(8,128)(2,1)S(1)}, u32[]{:S(2)}, u32[]{:S(2)}) collective-permute-start(bf16[8,32,128]{2,1,0:T(8,128)(2,1)S(1)} %get-tuple-element.34), channel_id=1, source_target_pairs={{0,4},{4,8},{8,12},{12,16},{16,20},{20,24},{24,28},{1,5},{5,9},{9,... | collective-permute-start | bytes 196616 | tf_op jit(solution)/shard_map/ppermute | solution.py:161
  6.2 0.0 copy-start.3
  6.2 1.4 %collective-permute-start.1 = (bf16[8,32,128]{2,1,0:T(8,128)(2,1)S(1)}, bf16[8,32,128]{2,1,0:T(8,128)(2,1)S(1)}, u32[]{:S(2)}, u32[]{:S(2)}) collective-permute-start(bf16[8,32,128]{2,1,0:T(8,128)(2,1)S(1)} %get-tuple-element.33), channel_id=1, source_target_pairs={{4,0},{8,4},{12,8},{16,12},{20,16},{24,20},{28,24},{5,1},{9,5},{13... | collective-permute-start | bytes 196616 | tf_op jit(solution)/shard_map/ppermute | solution.py:162
  7.6 0.0 copy-done.2
  7.7 0.0 copy-done.3
  7.7 0.0 copy-start
  7.8 3.1 %collective-permute-start.4 = (bf16[16,48,128]{2,1,0:T(8,128)(2,1)S(1)}, bf16[16,48,128]{2,1,0:T(8,128)(2,1)S(1)}, u32[]{:S(2)}, u32[]{:S(2)}) collective-permute-start(bf16[16,48,128]{2,1,0:T(8,128)(2,1)S(1)} %pad_maximum_fusion.b0), channel_id=1, source_target_pairs={{0,1},{1,2},{2,3},{3,0},{4,5},{5,6},{6,7},{7,4},{8,9},{9,10},{10,1... | collective-permute-start | bytes 589832 | tf_op jit(solution)/shard_map/ppermute | solution.py:189
  10.8 2.2 %collective-permute-start.5 = (bf16[16,48,128]{2,1,0:T(8,128)(2,1)S(1)}, bf16[16,48,128]{2,1,0:T(8,128)(2,1)S(1)}, u32[]{:S(2)}, u32[]{:S(2)}) collective-permute-start(bf16[16,48,128]{2,1,0:T(8,128)(2,1)S(1)} %pad_maximum_fusion.b0), channel_id=1, source_target_pairs={{0,3},{1,0},{2,1},{3,2},{4,7},{5,4},{6,5},{7,6},{8,11},{9,8},{10,9... | collective-permute-start | bytes 589832 | tf_op jit(solution)/shard_map/ppermute | solution.py:190
  13.0 0.0 copy-done
  13.1 0.2 copy.19.weight
  13.2 0.0 collective-permute-done.low
  13.2 0.0 collective-permute-done.1.high
  13.3 1.8 %shard_map.85 = bf16[4,16,32,128]{3,2,1,0:T(8,128)(2,1)} custom-call(bf16[8,32,128]{2,1,0:T(8,128)(2,1)S(1)} %collective-permute-done.low, bf16[16,32,128]{2,1,0:T(8,128)(2,1)S(1)} %bitcast.42, bf16[8,32,128]{2,1,0:T(8,128)(2,1)S(1)} %collective-permute-done.1.high, bf16[128,864]{1,0:T(8,128)(2,1)S(1)} %copy.19.weight), custom_call_target="tpu_custom_call" | custom-call | flops 2500000000 | bytes 1048576 | tf_op jit(solution)/shard_map/pallas_call | solution.py:193
  15.1 5.7 %all-to-all-start = ((bf16[4,16,32,128]{3,2,1,0:T(8,128)(2,1)}), bf16[4,16,32,128]{3,2,1,0:T(8,128)(2,1)S(1)}, u32[]{:S(2)}, u32[]{:S(2)}) async-start(bf16[4,16,32,128]{3,2,1,0:T(8,128)(2,1)} %shard_map.85), calls=%async_computation | async-start | bytes 1048576 | tf_op jit(solution)/shard_map/all_to_all | solution.py:196
  20.7 0.0 collective-permute-done.4.from_left.b1
  20.7 0.0 collective-permute-done.5.from_right.b2
  20.8 2.4 %collective-permute-start.6 = (bf16[8,48,128]{2,1,0:T(8,128)(2,1)S(1)}, bf16[8,48,128]{2,1,0:T(8,128)(2,1)S(1)}, u32[]{:S(2)}, u32[]{:S(2)}) collective-permute-start(bf16[8,48,128]{2,1,0:T(8,128)(2,1)S(1)} %get-tuple-element.17), channel_id=1, source_target_pairs={{0,1},{1,2},{2,3},{3,0},{4,5},{5,6},{6,7},{7,4},{8,9},{9,10},{10,1... | collective-permute-start | bytes 294920 | tf_op jit(solution)/shard_map/ppermute | solution.py:201
  23.2 1.3 %collective-permute-start.7 = (bf16[8,48,128]{2,1,0:T(8,128)(2,1)S(1)}, bf16[8,48,128]{2,1,0:T(8,128)(2,1)S(1)}, u32[]{:S(2)}, u32[]{:S(2)}) collective-permute-start(bf16[8,48,128]{2,1,0:T(8,128)(2,1)S(1)} %get-tuple-element.18), channel_id=1, source_target_pairs={{0,3},{1,0},{2,1},{3,2},{4,7},{5,4},{6,5},{7,6},{8,11},{9,8},{10,9... | collective-permute-start | bytes 294920 | tf_op jit(solution)/shard_map/ppermute | solution.py:202
  24.5 5.8 %all-to-all-done = bf16[4,16,32,128]{3,2,1,0:T(8,128)(2,1)S(1)} async-done(((bf16[4,16,32,128]{3,2,1,0:T(8,128)(2,1)}), bf16[4,16,32,128]{3,2,1,0:T(8,128)(2,1)S(1)}, u32[]{:S(2)}, u32[]{:S(2)}) %all-to-all-start) | async-done | bytes 524320 | tf_op jit(solution)/shard_map/all_to_all | solution.py:196
  30.3 0.1 convert_reduce_fusion
  30.4 0.1 select_convert_fusion.own
  30.5 5.1 %collective-permute-start.2 = (bf16[8,32,128]{2,1,0:T(8,128)(2,1)S(1)}, bf16[8,32,128]{2,1,0:T(8,128)(2,1)S(1)}, u32[]{:S(2)}, u32[]{:S(2)}) collective-permute-start(bf16[8,32,128]{2,1,0:T(8,128)(2,1)S(1)} %get-tuple-element.32), channel_id=1, source_target_pairs={{0,4},{4,8},{8,12},{12,16},{16,20},{20,24},{24,28},{1,5},{5,9},{9,... | collective-permute-start | bytes 196616 | tf_op jit(solution)/shard_map/ppermute | solution.py:161
  35.6 1.3 %collective-permute-start.3 = (bf16[8,32,128]{2,1,0:T(8,128)(2,1)S(1)}, bf16[8,32,128]{2,1,0:T(8,128)(2,1)S(1)}, u32[]{:S(2)}, u32[]{:S(2)}) collective-permute-start(bf16[8,32,128]{2,1,0:T(8,128)(2,1)S(1)} %get-tuple-element.31), channel_id=1, source_target_pairs={{4,0},{8,4},{12,8},{16,12},{20,16},{24,20},{28,24},{5,1},{9,5},{13... | collective-permute-start | bytes 196616 | tf_op jit(solution)/shard_map/ppermute | solution.py:162
  36.9 0.0 collective-permute-done.6.b3
  36.9 0.0 collective-permute-done.7.b4
  37.0 1.3 %shard_map.87.filter_two = bf16[864,128]{1,0:T(8,128)(2,1)S(1)} custom-call(s32[1]{0:T(128)} %bitcast.me, bf16[8,32,128]{2,1,0:T(8,128)(2,1)S(1)} %collective-permute-done.low, bf16[16,32,128]{2,1,0:T(8,128)(2,1)S(1)} %bitcast.43, bf16[8,32,128]{2,1,0:T(8,128)(2,1)S(1)} %collective-permute-done.1.high, bf16[16,48,128]{2,1,0:T(8,128)(2,1)S(1)} %pad_maximum_fusion.b0, ...), custom_call_target="tpu_custom_call" | custom-call | flops 500000000 | bytes 1048576 | tf_op jit(solution)/shard_map/pallas_call | solution.py:208
  38.3 0.0 collective-permute-done.2.low
  38.3 4.3 %collective-permute-done.3.high = bf16[8,32,128]{2,1,0:T(8,128)(2,1)S(1)} collective-permute-done((bf16[8,32,128]{2,1,0:T(8,128)(2,1)S(1)}, bf16[8,32,128]{2,1,0:T(8,128)(2,1)S(1)}, u32[]{:S(2)}, u32[]{:S(2)}) %collective-permute-start.3) | collective-permute-done | bytes 65568 | tf_op jit(solution)/shard_map/ppermute | solution.py:162
  42.5 1.3 %shard_map.88 = bf16[1536,128]{1,0:T(8,128)(2,1)S(1)} custom-call(s32[1]{0:T(128)} %bitcast.me, bf16[8,32,128]{2,1,0:T(8,128)(2,1)S(1)} %collective-permute-done.2.low, bf16[16,32,128]{2,1,0:T(8,128)(2,1)S(1)} %select_convert_fusion.own, bf16[8,32,128]{2,1,0:T(8,128)(2,1)S(1)} %collective-permute-done.3.high, bf16[16,48,128]{2,1,0:T(8,128)(2,1)S(1)} %pad_maximum_fusion.b0, ...), custom_call_target="tpu_custom_call" | custom-call | flops 500000000 | bytes 1048576 | tf_op jit(solution)/shard_map/pallas_call | solution.py:217
  43.8 31.4 %all_to_all.15.pieces = bf16[64,24,128]{2,1,0:T(8,128)(2,1)S(1)} all-to-all(bf16[64,24,128]{2,1,0:T(8,128)(2,1)S(1)} %bitcast.44), channel_id=1, replica_groups=mesh['dp'=8,'space'=8,'chan'=4] {'dp','space'}, dimensions={0} | all-to-all | bytes 786432 | tf_op jit(solution)/shard_map/all_to_all | solution.py:228
  75.2 0.8 shard_map.90
  76.1 0.0 copy-start.1
  76.1 4.7 %all-to-all-start.2 = ((bf16[64,24,128]{2,1,0:T(8,128)(2,1)}), bf16[64,24,128]{2,1,0:T(8,128)(2,1)S(1)}, u32[]{:S(2)}, u32[]{:S(2)}) async-start(bf16[64,24,128]{2,1,0:T(8,128)(2,1)} %shard_map.90), calls=%async_computation.2 | async-start | bytes 786432 | tf_op jit(solution)/shard_map/all_to_all | solution.py:240
  80.8 0.0 copy-done.1
  80.8 0.1 copy.21
  80.9 0.1 fusion.weight
  81.0 1.0 %shard_map.89 = (f32[16,16,128]{2,1,0:T(8,128)S(1)}, bf16[16,16,128]{2,1,0:T(8,128)(2,1)S(1)}, bf16[16,16,128]{2,1,0:T(8,128)(2,1)S(1)}, bf16[16,16,128]{2,1,0:T(8,128)(2,1)S(1)}) custom-call(bf16[8,32,128]{2,1,0:T(8,128)(2,1)S(1)} %collective-permute-done.2.low, bf16[16,32,128]{2,1,0:T(8,128)(2,1)S(1)} %select_convert_fusion.own, ...), custom_call_target="tpu_custom_call" | custom-call | flops 500000000 | bytes 1048576 | tf_op jit(solution)/shard_map/pallas_call | solution.py:231
  82.0 0.1 collective-permute-start.10
  82.1 3.4 %collective-permute-start.9 = (bf16[16,16,128]{2,1,0:T(8,128)(2,1)S(1)}, bf16[16,16,128]{2,1,0:T(8,128)(2,1)S(1)}, u32[]{:S(2)}, u32[]{:S(2)}) collective-permute-start(bf16[16,16,128]{2,1,0:T(8,128)(2,1)S(1)} %get-tuple-element.26), channel_id=1, source_target_pairs={{0,2},{1,3},{2,0},{3,1},{4,6},{5,7},{6,4},{7,5},{8,10},{9,11},{10,... | collective-permute-start | bytes 196616 | tf_op jit(solution)/shard_map/ppermute | solution.py:235
  85.6 0.0 collective-permute-start.8
  85.6 0.9 collective-permute-done.10
  86.4 4.0 %collective-permute-done.9 = bf16[16,16,128]{2,1,0:T(8,128)(2,1)S(1)} collective-permute-done((bf16[16,16,128]{2,1,0:T(8,128)(2,1)S(1)}, bf16[16,16,128]{2,1,0:T(8,128)(2,1)S(1)}, u32[]{:S(2)}, u32[]{:S(2)}) %collective-permute-start.9) | collective-permute-done | bytes 65568 | tf_op jit(solution)/shard_map/ppermute | solution.py:235
  90.4 2.0 %collective-permute-done.8 = bf16[16,16,128]{2,1,0:T(8,128)(2,1)S(1)} collective-permute-done((bf16[16,16,128]{2,1,0:T(8,128)(2,1)S(1)}, bf16[16,16,128]{2,1,0:T(8,128)(2,1)S(1)}, u32[]{:S(2)}, u32[]{:S(2)}) %collective-permute-start.8) | collective-permute-done | bytes 65568 | tf_op jit(solution)/shard_map/ppermute | solution.py:236
  92.5 0.6 copy.28
  93.1 0.6 all-to-all-done.2
  93.7 1.0 %shard_map.91 = (f32[864,128]{1,0:T(8,128)}, f32[864,64]{1,0:T(8,128)}) custom-call(bf16[1536,128]{1,0:T(8,128)(2,1)S(1)} %bitcast.40), custom_call_target="tpu_custom_call" | custom-call | bytes 1048576 | tf_op jit(solution)/shard_map/pallas_call | solution.py:241
  (9 shorter events, 0.2 us)
Async XLA Ops:
  1.7 6.0 %copy-start.2 = (bf16[1,32,2,8,128]{4,3,2,1,0:T(8,128)(2,1)S(1)}, bf16[1,32,2,8,128]{4,3,2,1,0:T(8,128)(2,1)}, u32[]{:S(2)}) copy-start(bf16[1,32,2,8,128]{4,3,2,1,0:T(8,128)(2,1)} %param.7) | copy-start | bytes 393220
  1.7 11.6 %collective-permute-start = (bf16[8,32,128]{2,1,0:T(8,128)(2,1)S(1)}, bf16[8,32,128]{2,1,0:T(8,128)(2,1)S(1)}, u32[]{:S(2)}, u32[]{:S(2)}) collective-permute-start(bf16[8,32,128]{2,1,0:T(8,128)(2,1)S(1)} %get-tuple-element.34), channel_id=1, source_target_pairs={{0,4},{4,8},{8,12},{12,16},{16,20},{20,24},{24,28},{1,5},{5,9},{9,... | collective-permute-start | bytes 196616 | tf_op jit(solution)/shard_map/ppermute | solution.py:161
  6.2 1.5 %copy-start.3 = (bf16[1,16,2,8,128]{4,3,2,1,0:T(8,128)(2,1)S(1)}, bf16[1,16,2,8,128]{4,3,2,1,0:T(8,128)(2,1)}, u32[]{:S(2)}) copy-start(bf16[1,16,2,8,128]{4,3,2,1,0:T(8,128)(2,1)} %param.6) | copy-start | bytes 196612
  6.2 7.0 %collective-permute-start.1 = (bf16[8,32,128]{2,1,0:T(8,128)(2,1)S(1)}, bf16[8,32,128]{2,1,0:T(8,128)(2,1)S(1)}, u32[]{:S(2)}, u32[]{:S(2)}) collective-permute-start(bf16[8,32,128]{2,1,0:T(8,128)(2,1)S(1)} %get-tuple-element.33), channel_id=1, source_target_pairs={{4,0},{8,4},{12,8},{16,12},{20,16},{24,20},{28,24},{5,1},{9,5},{13... | collective-permute-start | bytes 196616 | tf_op jit(solution)/shard_map/ppermute | solution.py:162
  7.7 5.3 %copy-start = (bf16[32,27,128]{2,0,1:T(8,128)(2,1)S(1)}, bf16[32,27,128]{2,0,1:T(8,128)(2,1)}, u32[]{:S(2)}) copy-start(bf16[32,27,128]{2,0,1:T(8,128)(2,1)} %param.11) | copy-start | bytes 663556
  7.8 13.0 %collective-permute-start.4 = (bf16[16,48,128]{2,1,0:T(8,128)(2,1)S(1)}, bf16[16,48,128]{2,1,0:T(8,128)(2,1)S(1)}, u32[]{:S(2)}, u32[]{:S(2)}) collective-permute-start(bf16[16,48,128]{2,1,0:T(8,128)(2,1)S(1)} %pad_maximum_fusion.b0), channel_id=1, source_target_pairs={{0,1},{1,2},{2,3},{3,0},{4,5},{5,6},{6,7},{7,4},{8,9},{9,10},{10,1... | collective-permute-start | bytes 589832 | tf_op jit(solution)/shard_map/ppermute | solution.py:189
  10.8 9.9 %collective-permute-start.5 = (bf16[16,48,128]{2,1,0:T(8,128)(2,1)S(1)}, bf16[16,48,128]{2,1,0:T(8,128)(2,1)S(1)}, u32[]{:S(2)}, u32[]{:S(2)}) collective-permute-start(bf16[16,48,128]{2,1,0:T(8,128)(2,1)S(1)} %pad_maximum_fusion.b0), channel_id=1, source_target_pairs={{0,3},{1,0},{2,1},{3,2},{4,7},{5,4},{6,5},{7,6},{8,11},{9,8},{10,9... | collective-permute-start | bytes 589832 | tf_op jit(solution)/shard_map/ppermute | solution.py:190
  15.1 15.3 %all-to-all-start = ((bf16[4,16,32,128]{3,2,1,0:T(8,128)(2,1)}), bf16[4,16,32,128]{3,2,1,0:T(8,128)(2,1)S(1)}, u32[]{:S(2)}, u32[]{:S(2)}) async-start(bf16[4,16,32,128]{3,2,1,0:T(8,128)(2,1)} %shard_map.85), calls=%async_computation | async-start | bytes 1048576 | tf_op jit(solution)/shard_map/all_to_all | solution.py:196
  20.8 16.2 %collective-permute-start.6 = (bf16[8,48,128]{2,1,0:T(8,128)(2,1)S(1)}, bf16[8,48,128]{2,1,0:T(8,128)(2,1)S(1)}, u32[]{:S(2)}, u32[]{:S(2)}) collective-permute-start(bf16[8,48,128]{2,1,0:T(8,128)(2,1)S(1)} %get-tuple-element.17), channel_id=1, source_target_pairs={{0,1},{1,2},{2,3},{3,0},{4,5},{5,6},{6,7},{7,4},{8,9},{9,10},{10,1... | collective-permute-start | bytes 294920 | tf_op jit(solution)/shard_map/ppermute | solution.py:201
  23.2 13.8 %collective-permute-start.7 = (bf16[8,48,128]{2,1,0:T(8,128)(2,1)S(1)}, bf16[8,48,128]{2,1,0:T(8,128)(2,1)S(1)}, u32[]{:S(2)}, u32[]{:S(2)}) collective-permute-start(bf16[8,48,128]{2,1,0:T(8,128)(2,1)S(1)} %get-tuple-element.18), channel_id=1, source_target_pairs={{0,3},{1,0},{2,1},{3,2},{4,7},{5,4},{6,5},{7,6},{8,11},{9,8},{10,9... | collective-permute-start | bytes 294920 | tf_op jit(solution)/shard_map/ppermute | solution.py:202
  30.5 7.8 %collective-permute-start.2 = (bf16[8,32,128]{2,1,0:T(8,128)(2,1)S(1)}, bf16[8,32,128]{2,1,0:T(8,128)(2,1)S(1)}, u32[]{:S(2)}, u32[]{:S(2)}) collective-permute-start(bf16[8,32,128]{2,1,0:T(8,128)(2,1)S(1)} %get-tuple-element.32), channel_id=1, source_target_pairs={{0,4},{4,8},{8,12},{12,16},{16,20},{20,24},{24,28},{1,5},{5,9},{9,... | collective-permute-start | bytes 196616 | tf_op jit(solution)/shard_map/ppermute | solution.py:161
  35.6 6.9 %collective-permute-start.3 = (bf16[8,32,128]{2,1,0:T(8,128)(2,1)S(1)}, bf16[8,32,128]{2,1,0:T(8,128)(2,1)S(1)}, u32[]{:S(2)}, u32[]{:S(2)}) collective-permute-start(bf16[8,32,128]{2,1,0:T(8,128)(2,1)S(1)} %get-tuple-element.31), channel_id=1, source_target_pairs={{4,0},{8,4},{12,8},{16,12},{20,16},{24,20},{28,24},{5,1},{9,5},{13... | collective-permute-start | bytes 196616 | tf_op jit(solution)/shard_map/ppermute | solution.py:162
  76.1 4.7 %copy-start.1 = (bf16[32,27,64]{2,0,1:T(8,128)(2,1)S(1)}, bf16[32,27,64]{2,0,1:T(8,128)(2,1)}, u32[]{:S(2)}) copy-start(bf16[32,27,64]{2,0,1:T(8,128)(2,1)} %param.10) | copy-start | bytes 331780
  76.1 17.6 %all-to-all-start.2 = ((bf16[64,24,128]{2,1,0:T(8,128)(2,1)}), bf16[64,24,128]{2,1,0:T(8,128)(2,1)S(1)}, u32[]{:S(2)}, u32[]{:S(2)}) async-start(bf16[64,24,128]{2,1,0:T(8,128)(2,1)} %shard_map.90), calls=%async_computation.2 | async-start | bytes 786432 | tf_op jit(solution)/shard_map/all_to_all | solution.py:240
  82.0 4.4 %collective-permute-start.10 = (bf16[16,16,128]{2,1,0:T(8,128)(2,1)S(1)}, bf16[16,16,128]{2,1,0:T(8,128)(2,1)S(1)}, u32[]{:S(2)}, u32[]{:S(2)}) collective-permute-start(bf16[16,16,128]{2,1,0:T(8,128)(2,1)S(1)} %get-tuple-element.27), channel_id=1, source_target_pairs={{0,3},{1,0},{2,1},{3,2},{4,7},{5,4},{6,5},{7,6},{8,11},{9,8},{10,9... | collective-permute-start | bytes 196616 | tf_op jit(solution)/shard_map/ppermute | solution.py:237
  82.1 8.3 %collective-permute-start.9 = (bf16[16,16,128]{2,1,0:T(8,128)(2,1)S(1)}, bf16[16,16,128]{2,1,0:T(8,128)(2,1)S(1)}, u32[]{:S(2)}, u32[]{:S(2)}) collective-permute-start(bf16[16,16,128]{2,1,0:T(8,128)(2,1)S(1)} %get-tuple-element.26), channel_id=1, source_target_pairs={{0,2},{1,3},{2,0},{3,1},{4,6},{5,7},{6,4},{7,5},{8,10},{9,11},{10,... | collective-permute-start | bytes 196616 | tf_op jit(solution)/shard_map/ppermute | solution.py:235
  85.6 6.9 %collective-permute-start.8 = (bf16[16,16,128]{2,1,0:T(8,128)(2,1)S(1)}, bf16[16,16,128]{2,1,0:T(8,128)(2,1)S(1)}, u32[]{:S(2)}, u32[]{:S(2)}) collective-permute-start(bf16[16,16,128]{2,1,0:T(8,128)(2,1)S(1)} %get-tuple-element.25), channel_id=1, source_target_pairs={{0,1},{1,2},{2,3},{3,0},{4,5},{5,6},{6,7},{7,4},{8,9},{9,10},{10,1... | collective-permute-start | bytes 196616 | tf_op jit(solution)/shard_map/ppermute | solution.py:236

commit v4 on v3

--- a/solution.py
+++ b/solution.py
@@ -195,15 +195,16 @@
     )(low_two, delta_two, high_two, flipped(weight_two))
     parts = lax.all_to_all(partial_two, "chan", 0, 0, tiled=True)
 
-    halves = call(pass_kernel, (jax.ShapeDtypeStruct((8, 48, LANES), bf16),) * 2, [], 11_000_000_000, 2)(
+    halves = call(pass_kernel, (jax.ShapeDtypeStruct((8, 48, LANES), bf16),) * 2, [], 15_500_000_000, 2)(
         from_left, from_right
     )
-    far_first = lax.ppermute(halves[0], "chan", to_right)
-    far_second = lax.ppermute(halves[1], "chan", to_left)
-    blocks = (both, from_left, from_right, far_first, far_second)
-
     hidden_grad = jnp.sum(parts.astype(jnp.float32), axis=0)
     delta_one = jnp.where(hidden > 0, hidden_grad, jnp.zeros_like(hidden_grad)).astype(bf16)
+    first_half, second_half, delta_one = lax.optimization_barrier((*halves, delta_one))
+    far_first = lax.ppermute(first_half, "chan", to_right)
+    far_second = lax.ppermute(second_half, "chan", to_left)
+    blocks = (both, from_left, from_right, far_first, far_second)
+
     low_one, high_one = neighbours(delta_one[:8], delta_one[8:])
     filter_two = call(
         filter_two_kernel,

time: 95.5 us -> 95.3 us (level)
  waiting for transfers between devices: 17.6 us -> 22.2 us
  blocking collectives: 31.4 us -> 27.7 us
    all_to_all x1, waiting for transfers between devices: 5.85 us -> 9.58 us  [local(): parts = lax.all_to_all(partial_two, 'chan', 0, 0, tiled=True)]
    all_to_all x1, blocking collectives: 31.4 us -> 27.7 us  [local(): lax.all_to_all(sums.reshape(64, CHUNK, LANES), every, 0, 0, tiled=True)]
    ppermute x1, starting transfers between devices: 0.01 us -> 2.35 us  [local(): right = lax.ppermute(right, 'chan', to_right)]
    ppermute x1, starting transfers between devices: 3.44 us -> 1.51 us  [local(): across = lax.ppermute(across, 'chan', [(i, (i + 2) % 4) for i in range(4)])]
    ppermute x2, waiting for transfers between devices: 4.27 us -> 5.51 us  [neighbours(): high = lax.ppermute(first, 'space', backward)]
    ppermute x1, waiting for transfers between devices: 3.97 us -> 5.09 us  [local(): across = lax.ppermute(across, 'chan', [(i, (i + 2) % 4) for i in range(4)])]
    ppermute x2, starting transfers between devices: 9.64 us -> 8.57 us  [neighbours(): low = lax.ppermute(second, 'space', forward)]
  transfers between devices with their start and end apart: 13 -> 13, of which waited for: 6 -> 5; matrix products, arithmetic and copies ran while one was open for 1% -> 1% of each run, Pallas kernels for 4% -> 4%
where the time goes in v4:
time: 95.3 us; the launch traced here: 94.9 us
  starting transfers between devices  34.5 us (36%)
  blocking collectives  27.7 us (29%)
  waiting for transfers between devices  22.2 us (23%)
  Pallas kernels  7.23 us (8%)
  other arithmetic  1.31 us (1%)
  local copies, waits for them, and re-layouts  1.05 us (1%)
    all_to_all x1, blocking collectives, local(): lax.all_to_all(sums.reshape(64, CHUNK, LANES), every, 0, 0, tiled=True)  27.7 us
    all_to_all x1, waiting for transfers between devices, local(): parts = lax.all_to_all(partial_two, 'chan', 0, 0, tiled=True)  9.58 us
    ppermute x2, starting transfers between devices, neighbours(): low = lax.ppermute(second, 'space', forward)  8.57 us
    all_to_all x1, starting transfers between devices, local(): parts = lax.all_to_all(partial_two, 'chan', 0, 0, tiled=True)  5.65 us
    ppermute x2, waiting for transfers between devices, neighbours(): high = lax.ppermute(first, 'space', backward)  5.51 us
    ppermute x1, waiting for transfers between devices, local(): across = lax.ppermute(across, 'chan', [(i, (i + 2) % 4) for i in range(4)])  5.09 us
    all_to_all x1, starting transfers between devices, local(): lax.all_to_all(copies, every, 0, 0, tiled=True).reshape(64 * CHUNK, LANES)  4.66 us
    ppermute x1, starting transfers between devices, local(): far_second = lax.ppermute(second_half, 'chan', to_left)  3.47 us
  transfers between devices with their start and end apart: 13, of which 5 were waited for; matrix products, arithmetic and copies ran while one was open for 1% of the time, Pallas kernels for 4%

profile of v4, /device:TPU:1, one launch (start us, length us, event | category | flops | bytes accessed | tf_op | source)
XLA Modules:
  0.0 94.9 jit_solution(3241372413353465966)
XLA Ops:
  0.6 1.0 %compare_select_fusion = bf16[1,32,2,8,128]{4,1,3,2,0:T(8,128)(2,1)S(1)} fusion(bf16[1,32,2,8,128]{4,3,2,1,0:T(8,128)(2,1)} %param.9, bf16[1,32,2,8,128]{4,3,2,1,0:T(8,128)(2,1)} %param.8), kind=kLoop, calls=%fused_computation.2 | loop fusion | flops 131072 | bytes 393216 | tf_op jit(solution)/shard_map/jit(_where)/select_n | solution.py:183
  1.7 0.0 copy-start.2
  1.7 4.5 %collective-permute-start.2 = (bf16[8,32,128]{2,1,0:T(8,128)(2,1)S(1)}, bf16[8,32,128]{2,1,0:T(8,128)(2,1)S(1)}, u32[]{:S(2)}, u32[]{:S(2)}) collective-permute-start(bf16[8,32,128]{2,1,0:T(8,128)(2,1)S(1)} %get-tuple-element.40), channel_id=1, source_target_pairs={{0,4},{4,8},{8,12},{12,16},{16,20},{20,24},{24,28},{1,5},{5,9},{9,... | collective-permute-start | bytes 196616 | tf_op jit(solution)/shard_map/ppermute | solution.py:161
  6.2 0.0 copy-start.3
  6.2 1.4 %collective-permute-start.3 = (bf16[8,32,128]{2,1,0:T(8,128)(2,1)S(1)}, bf16[8,32,128]{2,1,0:T(8,128)(2,1)S(1)}, u32[]{:S(2)}, u32[]{:S(2)}) collective-permute-start(bf16[8,32,128]{2,1,0:T(8,128)(2,1)S(1)} %get-tuple-element.39), channel_id=1, source_target_pairs={{4,0},{8,4},{12,8},{16,12},{20,16},{24,20},{28,24},{5,1},{9,5},{13... | collective-permute-start | bytes 196616 | tf_op jit(solution)/shard_map/ppermute | solution.py:162
  7.6 0.0 copy-done.2
  7.7 0.0 copy-done.3
  7.7 0.0 copy-start
  7.8 3.1 %collective-permute-start = (bf16[16,48,128]{2,1,0:T(8,128)(2,1)S(1)}, bf16[16,48,128]{2,1,0:T(8,128)(2,1)S(1)}, u32[]{:S(2)}, u32[]{:S(2)}) collective-permute-start(bf16[16,48,128]{2,1,0:T(8,128)(2,1)S(1)} %pad_maximum_fusion.b0), channel_id=1, source_target_pairs={{0,1},{1,2},{2,3},{3,0},{4,5},{5,6},{6,7},{7,4},{8,9},{9,10},{10,1... | collective-permute-start | bytes 589832 | tf_op jit(solution)/shard_map/ppermute | solution.py:189
  10.8 2.2 %collective-permute-start.1 = (bf16[16,48,128]{2,1,0:T(8,128)(2,1)S(1)}, bf16[16,48,128]{2,1,0:T(8,128)(2,1)S(1)}, u32[]{:S(2)}, u32[]{:S(2)}) collective-permute-start(bf16[16,48,128]{2,1,0:T(8,128)(2,1)S(1)} %pad_maximum_fusion.b0), channel_id=1, source_target_pairs={{0,3},{1,0},{2,1},{3,2},{4,7},{5,4},{6,5},{7,6},{8,11},{9,8},{10,9... | collective-permute-start | bytes 589832 | tf_op jit(solution)/shard_map/ppermute | solution.py:190
  13.0 0.0 copy-done
  13.1 0.2 copy.20.weight
  13.2 0.0 collective-permute-done.2.low
  13.2 0.0 collective-permute-done.3.high
  13.3 1.8 %shard_map.86 = bf16[4,16,32,128]{3,2,1,0:T(8,128)(2,1)} custom-call(bf16[8,32,128]{2,1,0:T(8,128)(2,1)S(1)} %collective-permute-done.2.low, bf16[16,32,128]{2,1,0:T(8,128)(2,1)S(1)} %bitcast.42, bf16[8,32,128]{2,1,0:T(8,128)(2,1)S(1)} %collective-permute-done.3.high, bf16[128,864]{1,0:T(8,128)(2,1)S(1)} %copy.20.weight), custom_call_target="tpu_custom_call" | custom-call | flops 2500000000 | bytes 1048576 | tf_op jit(solution)/shard_map/pallas_call | solution.py:193
  15.1 5.7 %all-to-all-start = ((bf16[4,16,32,128]{3,2,1,0:T(8,128)(2,1)}), bf16[4,16,32,128]{3,2,1,0:T(8,128)(2,1)S(1)}, u32[]{:S(2)}, u32[]{:S(2)}) async-start(bf16[4,16,32,128]{3,2,1,0:T(8,128)(2,1)} %shard_map.86), calls=%async_computation | async-start | bytes 1048576 | tf_op jit(solution)/shard_map/all_to_all | solution.py:196
  20.7 0.0 collective-permute-done.from_left.b1
  20.7 0.0 collective-permute-done.1.from_right.b2
  20.8 9.6 %all-to-all-done = bf16[4,16,32,128]{3,2,1,0:T(8,128)(2,1)S(1)} async-done(((bf16[4,16,32,128]{3,2,1,0:T(8,128)(2,1)}), bf16[4,16,32,128]{3,2,1,0:T(8,128)(2,1)S(1)}, u32[]{:S(2)}, u32[]{:S(2)}) %all-to-all-start) | async-done | bytes 524320 | tf_op jit(solution)/shard_map/all_to_all | solution.py:196
  30.3 0.1 convert_reduce_fusion
  30.4 0.1 select_convert_fusion.own
  30.5 0.2 collective-permute-start.6
  30.7 3.5 %collective-permute-start.7 = (bf16[8,48,128]{2,1,0:T(8,128)(2,1)S(1)}, bf16[8,48,128]{2,1,0:T(8,128)(2,1)S(1)}, u32[]{:S(2)}, u32[]{:S(2)}) collective-permute-start(bf16[8,48,128]{2,1,0:T(8,128)(2,1)S(1)} %get-tuple-element.24), channel_id=1, source_target_pairs={{0,3},{1,0},{2,1},{3,2},{4,7},{5,4},{6,5},{7,6},{8,11},{9,8},{10,9... | collective-permute-start | bytes 294920 | tf_op jit(solution)/shard_map/ppermute | solution.py:205
  34.1 4.1 %collective-permute-start.4 = (bf16[8,32,128]{2,1,0:T(8,128)(2,1)S(1)}, bf16[8,32,128]{2,1,0:T(8,128)(2,1)S(1)}, u32[]{:S(2)}, u32[]{:S(2)}) collective-permute-start(bf16[8,32,128]{2,1,0:T(8,128)(2,1)S(1)} %get-tuple-element.38), channel_id=1, source_target_pairs={{0,4},{4,8},{8,12},{12,16},{16,20},{20,24},{24,28},{1,5},{5,9},{9,... | collective-permute-start | bytes 196616 | tf_op jit(solution)/shard_map/ppermute | solution.py:161
  38.2 1.3 %collective-permute-start.5 = (bf16[8,32,128]{2,1,0:T(8,128)(2,1)S(1)}, bf16[8,32,128]{2,1,0:T(8,128)(2,1)S(1)}, u32[]{:S(2)}, u32[]{:S(2)}) collective-permute-start(bf16[8,32,128]{2,1,0:T(8,128)(2,1)S(1)} %get-tuple-element.37), channel_id=1, source_target_pairs={{4,0},{8,4},{12,8},{16,12},{20,16},{24,20},{28,24},{5,1},{9,5},{13... | collective-permute-start | bytes 196616 | tf_op jit(solution)/shard_map/ppermute | solution.py:162
  39.5 0.0 collective-permute-done.6.b3
  39.5 0.0 collective-permute-done.7.b4
  39.5 1.3 %shard_map.87.filter_two = bf16[864,128]{1,0:T(8,128)(2,1)S(1)} custom-call(s32[1]{0:T(128)} %bitcast.me, bf16[8,32,128]{2,1,0:T(8,128)(2,1)S(1)} %collective-permute-done.2.low, bf16[16,32,128]{2,1,0:T(8,128)(2,1)S(1)} %bitcast.43, bf16[8,32,128]{2,1,0:T(8,128)(2,1)S(1)} %collective-permute-done.3.high, bf16[16,48,128]{2,1,0:T(8,128)(2,1)S(1)} %pad_maximum_fusion.b0, ...), custom_call_target="tpu_custom_call" | custom-call | flops 500000000 | bytes 1048576 | tf_op jit(solution)/shard_map/pallas_call | solution.py:209
  40.8 0.0 collective-permute-done.4.low
  40.9 5.5 %collective-permute-done.5.high = bf16[8,32,128]{2,1,0:T(8,128)(2,1)S(1)} collective-permute-done((bf16[8,32,128]{2,1,0:T(8,128)(2,1)S(1)}, bf16[8,32,128]{2,1,0:T(8,128)(2,1)S(1)}, u32[]{:S(2)}, u32[]{:S(2)}) %collective-permute-start.5) | collective-permute-done | bytes 65568 | tf_op jit(solution)/shard_map/ppermute | solution.py:162
  46.4 1.3 %shard_map.88 = bf16[1536,128]{1,0:T(8,128)(2,1)S(1)} custom-call(s32[1]{0:T(128)} %bitcast.me, bf16[8,32,128]{2,1,0:T(8,128)(2,1)S(1)} %collective-permute-done.4.low, bf16[16,32,128]{2,1,0:T(8,128)(2,1)S(1)} %select_convert_fusion.own, bf16[8,32,128]{2,1,0:T(8,128)(2,1)S(1)} %collective-permute-done.5.high, bf16[16,48,128]{2,1,0:T(8,128)(2,1)S(1)} %pad_maximum_fusion.b0, ...), custom_call_target="tpu_custom_call" | custom-call | flops 500000000 | bytes 1048576 | tf_op jit(solution)/shard_map/pallas_call | solution.py:218
  47.7 27.7 %all_to_all.15.pieces = bf16[64,24,128]{2,1,0:T(8,128)(2,1)S(1)} all-to-all(bf16[64,24,128]{2,1,0:T(8,128)(2,1)S(1)} %bitcast.44), channel_id=1, replica_groups=mesh['dp'=8,'space'=8,'chan'=4] {'dp','space'}, dimensions={0} | all-to-all | bytes 786432 | tf_op jit(solution)/shard_map/all_to_all | solution.py:229
  75.4 0.8 shard_map.90
  76.2 0.0 copy-start.1
  76.2 4.7 %all-to-all-start.2 = ((bf16[64,24,128]{2,1,0:T(8,128)(2,1)}), bf16[64,24,128]{2,1,0:T(8,128)(2,1)S(1)}, u32[]{:S(2)}, u32[]{:S(2)}) async-start(bf16[64,24,128]{2,1,0:T(8,128)(2,1)} %shard_map.90), calls=%async_computation.2 | async-start | bytes 786432 | tf_op jit(solution)/shard_map/all_to_all | solution.py:241
  80.9 0.0 copy-done.1
  80.9 0.1 copy.21
  81.1 0.1 fusion.weight
  81.2 1.0 %shard_map.89 = (f32[16,16,128]{2,1,0:T(8,128)S(1)}, bf16[16,16,128]{2,1,0:T(8,128)(2,1)S(1)}, bf16[16,16,128]{2,1,0:T(8,128)(2,1)S(1)}, bf16[16,16,128]{2,1,0:T(8,128)(2,1)S(1)}) custom-call(bf16[8,32,128]{2,1,0:T(8,128)(2,1)S(1)} %collective-permute-done.4.low, bf16[16,32,128]{2,1,0:T(8,128)(2,1)S(1)} %select_convert_fusion.own, ...), custom_call_target="tpu_custom_call" | custom-call | flops 500000000 | bytes 1048576 | tf_op jit(solution)/shard_map/pallas_call | solution.py:232
  82.2 0.1 collective-permute-start.10
  82.3 2.4 %collective-permute-start.8 = (bf16[16,16,128]{2,1,0:T(8,128)(2,1)S(1)}, bf16[16,16,128]{2,1,0:T(8,128)(2,1)S(1)}, u32[]{:S(2)}, u32[]{:S(2)}) collective-permute-start(bf16[16,16,128]{2,1,0:T(8,128)(2,1)S(1)} %get-tuple-element.31), channel_id=1, source_target_pairs={{0,1},{1,2},{2,3},{3,0},{4,5},{5,6},{6,7},{7,4},{8,9},{9,10},{10,1... | collective-permute-start | bytes 196616 | tf_op jit(solution)/shard_map/ppermute | solution.py:237
  84.6 1.5 %collective-permute-start.9 = (bf16[16,16,128]{2,1,0:T(8,128)(2,1)S(1)}, bf16[16,16,128]{2,1,0:T(8,128)(2,1)S(1)}, u32[]{:S(2)}, u32[]{:S(2)}) collective-permute-start(bf16[16,16,128]{2,1,0:T(8,128)(2,1)S(1)} %get-tuple-element.32), channel_id=1, source_target_pairs={{0,2},{1,3},{2,0},{3,1},{4,6},{5,7},{6,4},{7,5},{8,10},{9,11},{10,... | collective-permute-start | bytes 196616 | tf_op jit(solution)/shard_map/ppermute | solution.py:236
  86.1 0.4 collective-permute-done.10
  86.6 1.6 %collective-permute-done.8 = bf16[16,16,128]{2,1,0:T(8,128)(2,1)S(1)} collective-permute-done((bf16[16,16,128]{2,1,0:T(8,128)(2,1)S(1)}, bf16[16,16,128]{2,1,0:T(8,128)(2,1)S(1)}, u32[]{:S(2)}, u32[]{:S(2)}) %collective-permute-start.8) | collective-permute-done | bytes 65568 | tf_op jit(solution)/shard_map/ppermute | solution.py:237
  88.1 5.1 %collective-permute-done.9 = bf16[16,16,128]{2,1,0:T(8,128)(2,1)S(1)} collective-permute-done((bf16[16,16,128]{2,1,0:T(8,128)(2,1)S(1)}, bf16[16,16,128]{2,1,0:T(8,128)(2,1)S(1)}, u32[]{:S(2)}, u32[]{:S(2)}) %collective-permute-start.9) | collective-permute-done | bytes 65568 | tf_op jit(solution)/shard_map/ppermute | solution.py:236
  93.3 0.6 copy.28
  93.9 0.0 all-to-all-done.2
  93.9 1.0 %shard_map.91 = (f32[864,128]{1,0:T(8,128)}, f32[864,64]{1,0:T(8,128)}) custom-call(bf16[1536,128]{1,0:T(8,128)(2,1)S(1)} %bitcast.40), custom_call_target="tpu_custom_call" | custom-call | bytes 1048576 | tf_op jit(solution)/shard_map/pallas_call | solution.py:242
  (9 shorter events, 0.2 us)
Async XLA Ops:
  1.7 6.0 %copy-start.2 = (bf16[1,32,2,8,128]{4,3,2,1,0:T(8,128)(2,1)S(1)}, bf16[1,32,2,8,128]{4,3,2,1,0:T(8,128)(2,1)}, u32[]{:S(2)}) copy-start(bf16[1,32,2,8,128]{4,3,2,1,0:T(8,128)(2,1)} %param.7) | copy-start | bytes 393220
  1.7 11.6 %collective-permute-start.2 = (bf16[8,32,128]{2,1,0:T(8,128)(2,1)S(1)}, bf16[8,32,128]{2,1,0:T(8,128)(2,1)S(1)}, u32[]{:S(2)}, u32[]{:S(2)}) collective-permute-start(bf16[8,32,128]{2,1,0:T(8,128)(2,1)S(1)} %get-tuple-element.40), channel_id=1, source_target_pairs={{0,4},{4,8},{8,12},{12,16},{16,20},{20,24},{24,28},{1,5},{5,9},{9,... | collective-permute-start | bytes 196616 | tf_op jit(solution)/shard_map/ppermute | solution.py:161
  6.2 1.5 %copy-start.3 = (bf16[1,16,2,8,128]{4,3,2,1,0:T(8,128)(2,1)S(1)}, bf16[1,16,2,8,128]{4,3,2,1,0:T(8,128)(2,1)}, u32[]{:S(2)}) copy-start(bf16[1,16,2,8,128]{4,3,2,1,0:T(8,128)(2,1)} %param.6) | copy-start | bytes 196612
  6.2 7.0 %collective-permute-start.3 = (bf16[8,32,128]{2,1,0:T(8,128)(2,1)S(1)}, bf16[8,32,128]{2,1,0:T(8,128)(2,1)S(1)}, u32[]{:S(2)}, u32[]{:S(2)}) collective-permute-start(bf16[8,32,128]{2,1,0:T(8,128)(2,1)S(1)} %get-tuple-element.39), channel_id=1, source_target_pairs={{4,0},{8,4},{12,8},{16,12},{20,16},{24,20},{28,24},{5,1},{9,5},{13... | collective-permute-start | bytes 196616 | tf_op jit(solution)/shard_map/ppermute | solution.py:162
  7.7 5.3 %copy-start = (bf16[32,27,128]{2,0,1:T(8,128)(2,1)S(1)}, bf16[32,27,128]{2,0,1:T(8,128)(2,1)}, u32[]{:S(2)}) copy-start(bf16[32,27,128]{2,0,1:T(8,128)(2,1)} %param.11) | copy-start | bytes 663556
  7.8 13.0 %collective-permute-start = (bf16[16,48,128]{2,1,0:T(8,128)(2,1)S(1)}, bf16[16,48,128]{2,1,0:T(8,128)(2,1)S(1)}, u32[]{:S(2)}, u32[]{:S(2)}) collective-permute-start(bf16[16,48,128]{2,1,0:T(8,128)(2,1)S(1)} %pad_maximum_fusion.b0), channel_id=1, source_target_pairs={{0,1},{1,2},{2,3},{3,0},{4,5},{5,6},{6,7},{7,4},{8,9},{9,10},{10,1... | collective-permute-start | bytes 589832 | tf_op jit(solution)/shard_map/ppermute | solution.py:189
  10.8 9.9 %collective-permute-start.1 = (bf16[16,48,128]{2,1,0:T(8,128)(2,1)S(1)}, bf16[16,48,128]{2,1,0:T(8,128)(2,1)S(1)}, u32[]{:S(2)}, u32[]{:S(2)}) collective-permute-start(bf16[16,48,128]{2,1,0:T(8,128)(2,1)S(1)} %pad_maximum_fusion.b0), channel_id=1, source_target_pairs={{0,3},{1,0},{2,1},{3,2},{4,7},{5,4},{6,5},{7,6},{8,11},{9,8},{10,9... | collective-permute-start | bytes 589832 | tf_op jit(solution)/shard_map/ppermute | solution.py:190
  15.1 15.3 %all-to-all-start = ((bf16[4,16,32,128]{3,2,1,0:T(8,128)(2,1)}), bf16[4,16,32,128]{3,2,1,0:T(8,128)(2,1)S(1)}, u32[]{:S(2)}, u32[]{:S(2)}) async-start(bf16[4,16,32,128]{3,2,1,0:T(8,128)(2,1)} %shard_map.86), calls=%async_computation | async-start | bytes 1048576 | tf_op jit(solution)/shard_map/all_to_all | solution.py:196
  30.5 9.0 %collective-permute-start.6 = (bf16[8,48,128]{2,1,0:T(8,128)(2,1)S(1)}, bf16[8,48,128]{2,1,0:T(8,128)(2,1)S(1)}, u32[]{:S(2)}, u32[]{:S(2)}) collective-permute-start(bf16[8,48,128]{2,1,0:T(8,128)(2,1)S(1)} %get-tuple-element.23), channel_id=1, source_target_pairs={{0,1},{1,2},{2,3},{3,0},{4,5},{5,6},{6,7},{7,4},{8,9},{9,10},{10,1... | collective-permute-start | bytes 294920 | tf_op jit(solution)/shard_map/ppermute | solution.py:204
  30.7 8.9 %collective-permute-start.7 = (bf16[8,48,128]{2,1,0:T(8,128)(2,1)S(1)}, bf16[8,48,128]{2,1,0:T(8,128)(2,1)S(1)}, u32[]{:S(2)}, u32[]{:S(2)}) collective-permute-start(bf16[8,48,128]{2,1,0:T(8,128)(2,1)S(1)} %get-tuple-element.24), channel_id=1, source_target_pairs={{0,3},{1,0},{2,1},{3,2},{4,7},{5,4},{6,5},{7,6},{8,11},{9,8},{10,9... | collective-permute-start | bytes 294920 | tf_op jit(solution)/shard_map/ppermute | solution.py:205
  34.1 6.7 %collective-permute-start.4 = (bf16[8,32,128]{2,1,0:T(8,128)(2,1)S(1)}, bf16[8,32,128]{2,1,0:T(8,128)(2,1)S(1)}, u32[]{:S(2)}, u32[]{:S(2)}) collective-permute-start(bf16[8,32,128]{2,1,0:T(8,128)(2,1)S(1)} %get-tuple-element.38), channel_id=1, source_target_pairs={{0,4},{4,8},{8,12},{12,16},{16,20},{20,24},{24,28},{1,5},{5,9},{9,... | collective-permute-start | bytes 196616 | tf_op jit(solution)/shard_map/ppermute | solution.py:161
  38.2 8.2 %collective-permute-start.5 = (bf16[8,32,128]{2,1,0:T(8,128)(2,1)S(1)}, bf16[8,32,128]{2,1,0:T(8,128)(2,1)S(1)}, u32[]{:S(2)}, u32[]{:S(2)}) collective-permute-start(bf16[8,32,128]{2,1,0:T(8,128)(2,1)S(1)} %get-tuple-element.37), channel_id=1, source_target_pairs={{4,0},{8,4},{12,8},{16,12},{20,16},{24,20},{28,24},{5,1},{9,5},{13... | collective-permute-start | bytes 196616 | tf_op jit(solution)/shard_map/ppermute | solution.py:162
  76.2 4.7 %copy-start.1 = (bf16[32,27,64]{2,0,1:T(8,128)(2,1)S(1)}, bf16[32,27,64]{2,0,1:T(8,128)(2,1)}, u32[]{:S(2)}) copy-start(bf16[32,27,64]{2,0,1:T(8,128)(2,1)} %param.10) | copy-start | bytes 331780
  76.2 17.7 %all-to-all-start.2 = ((bf16[64,24,128]{2,1,0:T(8,128)(2,1)}), bf16[64,24,128]{2,1,0:T(8,128)(2,1)S(1)}, u32[]{:S(2)}, u32[]{:S(2)}) async-start(bf16[64,24,128]{2,1,0:T(8,128)(2,1)} %shard_map.90), calls=%async_computation.2 | async-start | bytes 786432 | tf_op jit(solution)/shard_map/all_to_all | solution.py:241
  82.2 4.4 %collective-permute-start.10 = (bf16[16,16,128]{2,1,0:T(8,128)(2,1)S(1)}, bf16[16,16,128]{2,1,0:T(8,128)(2,1)S(1)}, u32[]{:S(2)}, u32[]{:S(2)}) collective-permute-start(bf16[16,16,128]{2,1,0:T(8,128)(2,1)S(1)} %get-tuple-element.33), channel_id=1, source_target_pairs={{0,3},{1,0},{2,1},{3,2},{4,7},{5,4},{6,5},{7,6},{8,11},{9,8},{10,9... | collective-permute-start | bytes 196616 | tf_op jit(solution)/shard_map/ppermute | solution.py:238
  82.3 5.9 %collective-permute-start.8 = (bf16[16,16,128]{2,1,0:T(8,128)(2,1)S(1)}, bf16[16,16,128]{2,1,0:T(8,128)(2,1)S(1)}, u32[]{:S(2)}, u32[]{:S(2)}) collective-permute-start(bf16[16,16,128]{2,1,0:T(8,128)(2,1)S(1)} %get-tuple-element.31), channel_id=1, source_target_pairs={{0,1},{1,2},{2,3},{3,0},{4,5},{5,6},{6,7},{7,4},{8,9},{9,10},{10,1... | collective-permute-start | bytes 196616 | tf_op jit(solution)/shard_map/ppermute | solution.py:237
  84.6 8.6 %collective-permute-start.9 = (bf16[16,16,128]{2,1,0:T(8,128)(2,1)S(1)}, bf16[16,16,128]{2,1,0:T(8,128)(2,1)S(1)}, u32[]{:S(2)}, u32[]{:S(2)}) collective-permute-start(bf16[16,16,128]{2,1,0:T(8,128)(2,1)S(1)} %get-tuple-element.32), channel_id=1, source_target_pairs={{0,2},{1,3},{2,0},{3,1},{4,6},{5,7},{6,4},{7,5},{8,10},{9,11},{10,... | collective-permute-start | bytes 196616 | tf_op jit(solution)/shard_map/ppermute | solution.py:236
